TPU v7x, 256 devices: a whole 4x4x8 slice. The times are simulated.
256 devices in a mesh: gx: 32 (over x, y, core), gy: 8 (over z).
Axes of the slice: x: 4, y: 4, z: 8, core: 2. Of those that a mesh axis runs over, the one named last changes fastest.
Arguments:
- points_x: bfloat16 [32, 16, 512, 256], P('gx', 'gy'), may hold values from -6 to 6
- near_tiles: bfloat16 [32, 16, 5, 512, 512], P('gx', 'gy'), may hold values from -0.09375 to 0.09375
- scales: float32 [32, 16, 5, 512], P('gx', 'gy'), may hold values from 0.25 to 4
- slot_direction: int32 [32, 16, 5], P('gx', 'gy'), may hold values from 0 to 4, each once within a row
- basis: bfloat16 [32, 16, 512, 256], P('gx', 'gy'), may hold values from -6 to 6
- leaf_transfer: float32 [32, 16, 256, 256], P('gx', 'gy'), may hold values from -1 to 2
- node_transfer: float32 [32, 8, 128, 256], P('gx', 'gy'), may hold values from -1 to 2
Outputs:
- near_field: bfloat16 [32, 16, 512, 256], P('gx', 'gy')
- leaf_q: bfloat16 [32, 16, 512, 256], P('gx', 'gy')
- top_factor: float32 [32, 8, 256, 256], P('gx', 'gy')
Inputs may be any that keep to these rules, and one draw needn't show every extreme that they name: `slot_direction`: each leaf's row names each of the five directions once.
All inputs are finite; a program needn't handle non-finite values.
Results may differ from a plain program's by a relative error of at most 0.0065.
Values may be sent and summed in bfloat16 or wider, within the bound.
No kernel may reach another device: no remote copies, remote signals or barrier semaphores. Data moves between devices by JAX's collectives and lax.ppermute only.
A program may use at most 128 MiB of HBM per device.

v0:
```python
import jax
import jax.numpy as jnp
from jax import lax
from jax.experimental import pallas as pl
from jax.experimental.pallas import tpu as pltpu
from jax.sharding import PartitionSpec as P

F32 = jnp.float32
BF16 = jnp.bfloat16
ANY = pl.BlockSpec(memory_space=pl.ANY)
VMEM = pl.BlockSpec(memory_space=pltpu.VMEM)
SMEM = pl.BlockSpec(memory_space=pltpu.SMEM)
PANEL = 32
PIECE = 16


def dot(a, b, dims, precision=lax.Precision.HIGHEST):
    return lax.dot_general(a, b, (dims, ((), ())), precision=precision, preferred_element_type=F32)


def nn(a, b):
    return dot(a, b, ((1,), (0,)))


def tn(a, b):
    return dot(a, b, ((0,), (0,)))


def bf_nn(a, b):
    return dot(a, b, ((1,), (0,)), lax.Precision.DEFAULT)


def bf_nt(a, b):
    return dot(a, b, ((1,), (1,)), lax.Precision.DEFAULT)


def swap(block, axes, sizes, partner):
    count_x, count_y = sizes
    route = []
    for i in range(count_x):
        for j in range(count_y):
            x, y = partner(i, j)
            if 0 <= x < count_x and 0 <= y < count_y:
                route.append((i * count_y + j, x * count_y + y))
    return lax.ppermute(block, axes, route)


def panel_step(k, tiles, nb, sb):
    iota = lax.broadcasted_iota(jnp.int32, (8, 128), 0)
    groups = nb // 8
    scale = [jnp.ones((8, 128), F32) for _ in range(groups)]
    for s in range(0, nb, sb):
        base = (k + s) % 128
        g0 = s // 8
        cols = []
        for j in range(sb):
            cols.append(
                {
                    g: jnp.broadcast_to(tiles[g][0][:, base + j : base + j + 1], (8, 128))
                    for g in range(g0 + j // 8, groups)
                }
            )
        for p in range(sb):
            gp = g0 + p // 8
            r = p % 8
            pivot = jnp.broadcast_to(cols[p][gp][r : r + 1, :], (8, 128))
            inv = 1.0 / pivot
            scale[gp] = jnp.where(iota == r, lax.rsqrt(pivot), scale[gp])
            for j in range(p + 1, sb):
                gj = g0 + j // 8
                t = jnp.broadcast_to(cols[p][gj][j % 8 : j % 8 + 1, :], (8, 128)) * inv
                for g in range(gj, groups):
                    cols[j][g] = cols[j][g] - cols[p][g] * t
            rows = [jnp.broadcast_to(t[r : r + 1, :], (8, 128)) * inv for t in tiles[gp]]
            for g in range(gp, groups):
                c = cols[p][g]
                if g == gp:
                    if r == 7:
                        continue
                    c = jnp.where(iota > r, c, 0.0)
                tiles[g] = [t - c * w for t, w in zip(tiles[g], rows)]
    return [[t * scale[g] for t in tiles[g]] for g in range(groups)]


def factorize(reads, u_refs, w_refs, n):
    lanes = lax.broadcasted_iota(jnp.int32, (8, 128), 1)
    sub = lax.broadcasted_iota(jnp.int32, (8, 128), 0)
    nb = PANEL
    for k in range(0, n, nb):
        lo = k // 128 * 128
        hi = (k + nb - 1) // 128 * 128 + 128
        for read, u, w in zip(reads, u_refs, w_refs):
            main = read(slice(k, k + nb), slice(lo, n))
            side = jnp.zeros((nb, hi), F32)
            if k:
                col = u[0:k, k : k + nb]
                main = main - tn(col, u[0:k, lo:n])
                if w is not None:
                    side = -tn(col, w[0:k, 0:hi])
            tiles = []
            for g in range(nb // 8):
                row = [main[8 * g : 8 * g + 8, c : c + 128] for c in range(0, n - lo, 128)]
                if w is not None:
                    more = [side[8 * g : 8 * g + 8, c : c + 128] for c in range(0, hi, 128)]
                    more[-1] = more[-1] + jnp.where(lanes == sub + (k + 8 * g - (hi - 128)), 1.0, 0.0)
                    row += more
                tiles.append(row)
            tiles = panel_step(k, tiles, nb, PIECE)
            na = (n - lo) // 128
            for g in range(nb // 8):
                first = k + 8 * g
                r = slice(first, first + 8)
                for i in range(na):
                    c = lo + 128 * i
                    t = tiles[g][i]
                    if c == lo:
                        t = jnp.where(lanes + c >= sub + first, t, 0.0)
                    u[r, c : c + 128] = t
                for c in range(0, lo, 128):
                    u[r, c : c + 128] = jnp.zeros((8, 128), F32)
                if w is not None:
                    for i, c in enumerate(range(0, hi, 128)):
                        w[r, c : c + 128] = tiles[g][na + i]
                    for c in range(hi, n, 128):
                        w[r, c : c + 128] = jnp.zeros((8, 128), F32)


def gram_kernel(basis, transfer, node, gram, sent):
    points = basis.shape[2]
    total = None
    for leaf in range(2):
        b = basis[0, leaf]
        g = dot(b, b, ((0,), (0,)), lax.Precision.DEFAULT) / points
        gram[leaf] = g
        t = transfer[0, leaf]
        part = tn(t, nn(g, t))
        total = part if total is None else total + part
    rank = total.shape[0]
    sent[0:rank, :] = total
    sent[rank : rank + node.shape[2], :] = node[0, 0]


def node_kernel(own, other, out, stacked):
    rank = own.shape[1]
    half = rank // 2
    parity = lax.axis_index("gx") % 2
    gram = 0.25 * (own[0:rank, :] + other[0:rank, :])
    mine = pl.multiple_of(parity * half, half)
    theirs = pl.multiple_of((1 - parity) * half, half)
    stacked[pl.ds(mine, half), :] = own[rank : rank + half, :]
    stacked[pl.ds(theirs, half), :] = other[rank : rank + half, :]
    t = stacked[...]
    out[...] = 0.25 * tn(t, nn(gram, t))


def leaf_kernel(gram, basis, q, u, w):
    n = gram.shape[1]
    reads = [lambda r, c, m=m: gram[m, r, c] for m in range(2)]
    factorize(reads, [u.at[m] for m in range(2)], [w.at[m] for m in range(2)], n)
    for leaf in range(2):
        rest = w[leaf]
        total = None
        for _ in range(3):
            part = rest.astype(BF16)
            rest = rest - part.astype(F32)
            term = bf_nt(basis[0, leaf], part)
            total = term if total is None else total + term
        q[0, leaf] = total.astype(BF16)


def top_kernel(own, other, out):
    n = own.shape[0]
    factorize([lambda r, c: own[r, c] + other[r, c]], [out.at[0, 0]], [None], n)


def slot_of(slots, leaf, direction):
    found = 0
    for s in range(5):
        found = found + jnp.where(slots[0, leaf, s] == direction, s, 0)
    return found


def scale_row(scales, slots, leaf, direction):
    return scales[0, leaf, pl.ds(slot_of(slots, leaf, direction), 1), :]


def mirror_kernel(slots, points, scales, tiles, acc, gx_a, gx_b, ns_a, ns_b, ne_a, ne_b, nw_a, nw_b,
                  held, xt, east, west, up, tile_sems, out_sems):
    order = [(0, 2), (0, 1), (0, 3), (0, 4), (1, 1), (1, 2), (1, 3), (1, 4), (0, 0), (1, 0)]
    copies = {}
    for leaf, d in order:
        place = leaf * 5 + d
        copies[leaf, d] = pltpu.make_async_copy(
            tiles.at[0, leaf, slot_of(slots, leaf, d)], held.at[place], tile_sems.at[place]
        )
        copies[leaf, d].start()
    for leaf in range(2):
        xt[leaf] = points[0, leaf].T
    even_x = lax.axis_index("gx") % 2 == 0
    even_y = lax.axis_index("gy") % 2 == 0
    waits = []

    def out_pair(first, second, a, b, even):
        one, two = out_sems.at[len(waits)], out_sems.at[len(waits) + 1]

        @pl.when(even)
        def _():
            pltpu.make_async_copy(first, a, one).start()
            pltpu.make_async_copy(second, b, two).start()

        @pl.when(jnp.logical_not(even))
        def _():
            pltpu.make_async_copy(second, a, one).start()
            pltpu.make_async_copy(first, b, two).start()

        waits.append(pltpu.make_async_copy(first, a, one))
        waits.append(pltpu.make_async_copy(second, b, two))

    def mirrored(leaf, d):
        copies[leaf, d].wait()
        scaled = (xt[leaf].astype(F32) * scale_row(scales, slots, leaf, d)).astype(BF16)
        return bf_nn(scaled, held[leaf * 5 + d])

    def direct(leaf, d, x):
        return bf_nt(x, held[leaf * 5 + d]) * scale_row(scales, slots, leaf, d)

    acc[1] = mirrored(0, 2)
    acc[0] = direct(0, 2, xt[1])
    east[0] = mirrored(0, 1).astype(BF16)
    east_one = mirrored(0, 3)
    west[0] = mirrored(0, 4).astype(BF16)
    east[1] = (east_one + mirrored(1, 1)).astype(BF16)
    east[2] = xt[1]
    west[1] = xt[0]
    west[2] = xt[1]
    out_pair(east, west, gx_a, gx_b, even_x)
    for i, (a, b) in enumerate(((ns_a, ns_b), (ne_a, ne_b), (nw_a, nw_b))):
        up[i] = mirrored(1, 2 + i).astype(BF16)
        out_pair(up.at[i], xt.at[0], a, b, even_y)
    for leaf in range(2):
        copies[leaf, 0].wait()
        acc[leaf] += direct(leaf, 0, xt[leaf])
    for w in waits:
        w.wait()


def near_kernel(slots, scales, tiles, acc, gx_a, gx_b, ns_a, ns_b, ne_a, ne_b, nw_a, nw_b, out,
                held, east, west, north, south, tile_sems, in_sems):
    order = [(0, 1), (0, 3), (0, 4), (1, 1), (1, 2), (1, 3), (1, 4)]
    even_x = lax.axis_index("gx") % 2 == 0
    even_y = lax.axis_index("gy") % 2 == 0
    waits = []

    def in_pair(first, second, a, b, even):
        one, two = in_sems.at[len(waits)], in_sems.at[len(waits) + 1]

        @pl.when(even)
        def _():
            pltpu.make_async_copy(a, first, one).start()
            pltpu.make_async_copy(b, second, two).start()

        @pl.when(jnp.logical_not(even))
        def _():
            pltpu.make_async_copy(b, first, one).start()
            pltpu.make_async_copy(a, second, two).start()

        waits.append(pltpu.make_async_copy(a, first, one))
        waits.append(pltpu.make_async_copy(b, second, two))

    in_pair(east, west, gx_a, gx_b, even_x)
    copies = {}
    for leaf, d in order:
        place = leaf * 5 + d
        copies[leaf, d] = pltpu.make_async_copy(
            tiles.at[0, leaf, slot_of(slots, leaf, d)], held.at[place], tile_sems.at[place]
        )
        copies[leaf, d].start()
    for i, (a, b) in enumerate(((ns_a, ns_b), (ne_a, ne_b), (nw_a, nw_b))):
        in_pair(north.at[i], south.at[i], a, b, even_y)
    for w in waits:
        w.wait()

    def direct(leaf, d, x):
        copies[leaf, d].wait()
        return bf_nt(x, held[leaf * 5 + d]) * scale_row(scales, slots, leaf, d)

    low = acc[0] + west[0].astype(F32)
    for i in range(3):
        low = low + south[i].astype(F32)
    low = low + direct(0, 1, east[1])
    low = low + direct(0, 3, east[2])
    low = low + direct(0, 4, west[2])
    out[0, 0] = low.T.astype(BF16)
    high = acc[1] + west[1].astype(F32) + east[0].astype(F32)
    high = high + direct(1, 1, east[2])
    for i in range(3):
        high = high + direct(1, 2 + i, north[i])
    out[0, 1] = high.T.astype(BF16)


def shape(*dims, dtype=BF16):
    return jax.ShapeDtypeStruct(dims, dtype)


def call(kernel, outs, in_specs, out_specs, scratch=(), flops=0, moved=0):
    return pl.pallas_call(
        kernel,
        out_shape=outs,
        in_specs=in_specs,
        out_specs=out_specs,
        scratch_shapes=list(scratch),
        compiler_params=pltpu.CompilerParams(vmem_limit_bytes=48 << 20),
        cost_estimate=pl.CostEstimate(flops=flops, bytes_accessed=moved, transcendentals=0),
    )


def make_shards(sizes):
    axes = ("gx", "gy")

    def shards(points_x, near_tiles, scales, slot_direction, basis, leaf_transfer, node_transfer):
        pts, vecs = points_x.shape[2:]
        rank = basis.shape[3]
        half = node_transfer.shape[2]
        dma = pltpu.SemaphoreType.DMA

        gram, sent = call(
            gram_kernel,
            (shape(2, rank, rank, dtype=F32), shape(rank + half, rank, dtype=F32)),
            [VMEM] * 3,
            (VMEM, VMEM),
            flops=10**9,
            moved=4 << 20,
        )(basis, leaf_transfer, node_transfer)
        got = swap(sent, axes, sizes, lambda i, j: (i ^ 1, j))

        block = shape(vecs, pts)
        trio = shape(3, vecs, pts)
        acc, *outgoing = call(
            mirror_kernel,
            (shape(2, vecs, pts, dtype=F32), trio, trio, *[block] * 6),
            [SMEM, VMEM, VMEM, ANY],
            (VMEM, *[ANY] * 8),
            [
                pltpu.VMEM((10, pts, pts), BF16),
                pltpu.VMEM((2, vecs, pts), BF16),
                pltpu.VMEM((3, vecs, pts), BF16),
                pltpu.VMEM((3, vecs, pts), BF16),
                pltpu.VMEM((3, vecs, pts), BF16),
                dma((10,)),
                dma((8,)),
            ],
            flops=3 * 10**9,
            moved=10 << 20,
        )(slot_direction, points_x, scales, near_tiles)

        node = call(node_kernel, shape(rank, rank, dtype=F32), [VMEM] * 2, VMEM,
                    [pltpu.VMEM((rank, rank), F32)], flops=10**9, moved=2 << 20)(sent, got)
        pair = node + swap(node, axes, sizes, lambda i, j: (i ^ 2, j))
        other = swap(pair, axes, sizes, lambda i, j: (i, j ^ 1))

        def across(parity, first):
            return lambda i, j: first(i, j, 1 if (j % 2 == 0) == (parity == 0) else -1)

        incoming = []
        for parity in range(2):
            incoming.append(
                swap(outgoing[parity], axes, sizes,
                     lambda i, j, q=parity: (i + (1 if (i % 2 == 0) == (q == 0) else -1), j))
            )
        for turn, side in enumerate((0, 1, -1)):
            for parity in range(2):
                incoming.append(
                    swap(outgoing[2 + 2 * turn + parity], axes, sizes,
                         across(parity, lambda i, j, step, side=side: (i + side * step, j + step)))
                )

        leaf_q = call(
            leaf_kernel,
            shape(*basis.shape),
            [VMEM] * 2,
            VMEM,
            [pltpu.VMEM((2, rank, rank), F32), pltpu.VMEM((2, rank, rank), F32)],
            flops=12 * 10**9,
            moved=4 << 20,
        )(gram, basis)

        top = call(top_kernel, shape(1, 1, rank, rank, dtype=F32), [VMEM] * 2, VMEM, flops=8 * 10**9,
                   moved=1 << 20)(pair, other)

        near = call(
            near_kernel,
            shape(*points_x.shape),
            [SMEM, VMEM, ANY, VMEM, *[ANY] * 8],
            VMEM,
            [
                pltpu.VMEM((10, pts, pts), BF16),
                *[pltpu.VMEM((3, vecs, pts), BF16)] * 4,
                dma((10,)),
                dma((8,)),
            ],
            flops=3 * 10**9,
            moved=10 << 20,
        )(slot_direction, scales, near_tiles, acc, *incoming)
        return near, leaf_q, top

    return shards


def solution(mesh):
    leaf = P("gx", "gy", None, None)
    placed = (leaf, P("gx", "gy", None, None, None), leaf, P("gx", "gy", None), leaf, leaf, leaf)
    return jax.shard_map(
        make_shards((mesh.shape["gx"], mesh.shape["gy"])),
        mesh=mesh,
        in_specs=placed,
        out_specs=(leaf, leaf, leaf),
        check_vma=False,
    )
```

profile of v0, /device:TPU:7, one launch (start us, length us, event | category | flops | bytes accessed | tf_op | source)
XLA Modules:
  0.0 69.5 jit_solution(11582358226842787081)
XLA Ops:
  0.6 0.0 copy-start
  0.6 1.0 %copy-done = f32[1,2,256,256]{3,2,1,0:T(8,128)S(1)} copy-done((f32[1,2,256,256]{3,2,1,0:T(8,128)S(1)}, f32[1,2,256,256]{3,2,1,0:T(8,128)}, u32[]{:S(2)}) %copy-start) | copy-done | bytes 524312
  1.7 0.0 copy-start.2
  1.7 1.0 %copy-done.2 = bf16[1,2,512,256]{3,2,1,0:T(8,128)(2,1)S(1)} copy-done((bf16[1,2,512,256]{3,2,1,0:T(8,128)(2,1)S(1)}, bf16[1,2,512,256]{3,2,1,0:T(8,128)(2,1)}, u32[]{:S(2)}) %copy-start.2) | copy-done | bytes 524312
  2.7 0.0 copy-start.4
  2.7 0.9 %copy-done.4 = f32[1,1,128,256]{3,2,1,0:T(8,128)S(1)} copy-done((f32[1,1,128,256]{3,2,1,0:T(8,128)S(1)}, f32[1,1,128,256]{3,2,1,0:T(8,128)}, u32[]{:S(2)}) %copy-start.4) | copy-done | bytes 131096
  3.6 2.2 %shard_map.96 = (f32[2,256,256]{2,1,0:T(8,128)S(1)}, f32[384,256]{1,0:T(8,128)S(1)}) custom-call(bf16[1,2,512,256]{3,2,1,0:T(8,128)(2,1)S(1)} %copy-done.2, f32[1,2,256,256]{3,2,1,0:T(8,128)S(1)} %copy-done, f32[1,1,128,256]{3,2,1,0:T(8,128)S(1)} %copy-done.4), custom_call_target="tpu_custom_call" | custom-call | flops 1000000000 | bytes 4194304 | tf_op jit(solution)/shard_map/pallas_call | solution.py:326
  5.8 0.8 %collective-permute-start.8 = (f32[384,256]{1,0:T(8,128)S(1)}, f32[384,256]{1,0:T(8,128)S(1)}, u32[]{:S(2)}, u32[]{:S(2)}) collective-permute-start(f32[384,256]{1,0:T(8,128)S(1)} %get-tuple-element.24.own), channel_id=1, source_target_pairs={{0,8},{1,9},{2,10},{3,11},{4,12},{5,13},{6,14},{7,15},{8,0},{9,1},... | collective-permute-start | bytes 1179656 | tf_op jit(solution)/shard_map/ppermute | solution.py:45
  6.6 0.7 %copy.11.scales = f32[1,2,5,512]{3,2,1,0:T(8,128)S(1)} copy(f32[1,2,5,512]{3,1,2,0:T(2,128)} %param.9) | data formatting | bytes 40960 | tf_op args[2]
  7.3 0.0 copy-start.1
  7.3 1.0 %copy-done.1 = bf16[1,2,512,256]{3,2,1,0:T(8,128)(2,1)S(1)} copy-done((bf16[1,2,512,256]{3,2,1,0:T(8,128)(2,1)S(1)}, bf16[1,2,512,256]{3,2,1,0:T(8,128)(2,1)}, u32[]{:S(2)}) %copy-start.1) | copy-done | bytes 524312
  8.3 0.0 copy-start.5
  8.3 0.7 copy-done.5
  9.0 0.0 copy-start.3
  9.0 5.3 %shard_map.94 = (f32[2,256,512]{2,1,0:T(8,128)S(1)}, bf16[3,256,512]{2,1,0:T(8,128)(2,1)S(1)}, bf16[3,256,512]{2,1,0:T(8,128)(2,1)S(1)}, bf16[256,512]{1,0:T(8,1...) custom-call(s32[1,2,5]{2,1,0:T(2,128)S(1)} %copy-done.5, ...), custom_call_target="tpu_custom_call" | custom-call | flops 3000000000 | bytes 10485760 | tf_op jit(solution)/shard_map/pallas_call | solution.py:338
  14.3 1.7 %collective-permute-start.2 = (bf16[256,512]{1,0:T(8,128)(2,1)S(1)}, bf16[256,512]{1,0:T(8,128)(2,1)S(1)}, u32[]{:S(2)}, u32[]{:S(2)}) collective-permute-start(bf16[256,512]{1,0:T(8,128)(2,1)S(1)} %get-tuple-element.17), channel_id=1, source_target_pairs={{0,1},{1,0},{2,3},{3,2},{4,5},{5,4},{6,7},{7,6},{8,9},{9,8},{10,11... | collective-permute-start | bytes 786440 | tf_op jit(solution)/shard_map/ppermute | solution.py:45
  16.0 0.7 collective-permute-start.3
  16.7 7.9 %collective-permute-start.4 = (bf16[256,512]{1,0:T(8,128)(2,1)S(1)}, bf16[256,512]{1,0:T(8,128)(2,1)S(1)}, u32[]{:S(2)}, u32[]{:S(2)}) collective-permute-start(bf16[256,512]{1,0:T(8,128)(2,1)S(1)} %get-tuple-element.19), channel_id=1, source_target_pairs={{0,9},{2,11},{4,13},{6,15},{8,17},{9,0},{10,19},{11,2},{12,21},{13... | collective-permute-start | bytes 786440 | tf_op jit(solution)/shard_map/ppermute | solution.py:45
  24.6 0.0 collective-permute-done.8.other
  24.6 1.1 %shard_map.98 = f32[256,256]{1,0:T(8,128)S(1)} custom-call(f32[384,256]{1,0:T(8,128)S(1)} %get-tuple-element.24.own, f32[384,256]{1,0:T(8,128)S(1)} %collective-permute-done.8.other), custom_call_target="tpu_custom_call" | custom-call | flops 1000000000 | bytes 2097152 | tf_op jit(solution)/shard_map/pallas_call | solution.py:356
  25.7 1.4 %collective-permute-start.9 = (f32[256,256]{1,0:T(8,128)S(1)}, f32[256,256]{1,0:T(8,128)S(1)}, u32[]{:S(2)}, u32[]{:S(2)}) collective-permute-start(f32[256,256]{1,0:T(8,128)S(1)} %shard_map.98), channel_id=1, source_target_pairs={{0,16},{1,17},{2,18},{3,19},{4,20},{5,21},{6,22},{7,23},{8,24},{9,... | collective-permute-start | bytes 786440 | tf_op jit(solution)/shard_map/ppermute | solution.py:45
  27.1 0.0 collective-permute-start
  27.1 0.0 collective-permute-done.2.ns_a
  27.1 2.5 %collective-permute-start.1 = (bf16[3,256,512]{2,1,0:T(8,128)(2,1)S(1)}, bf16[3,256,512]{2,1,0:T(8,128)(2,1)S(1)}, u32[]{:S(2)}, u32[]{:S(2)}) collective-permute-start(bf16[3,256,512]{2,1,0:T(8,128)(2,1)S(1)} %get-tuple-element.16), channel_id=1, source_target_pairs={{8,16},{9,17},{10,18},{11,19},{12,20},{13,21},{14,22},{15,23},{16,... | collective-permute-start | bytes 2359304 | tf_op jit(solution)/shard_map/ppermute | solution.py:45
  29.6 0.0 collective-permute-done.3.ns_b
  29.6 0.7 collective-permute-start.5
  30.3 0.5 collective-permute-done.4.ne_a
  30.8 6.5 %collective-permute-start.6 = (bf16[256,512]{1,0:T(8,128)(2,1)S(1)}, bf16[256,512]{1,0:T(8,128)(2,1)S(1)}, u32[]{:S(2)}, u32[]{:S(2)}) collective-permute-start(bf16[256,512]{1,0:T(8,128)(2,1)S(1)} %get-tuple-element.21), channel_id=1, source_target_pairs={{1,8},{3,10},{5,12},{7,14},{8,1},{9,16},{10,3},{11,18},{12,5},{13,... | collective-permute-start | bytes 786440 | tf_op jit(solution)/shard_map/ppermute | solution.py:45
  37.3 0.0 collective-permute-done.9
  37.3 0.9 %collective-permute-start.7 = (bf16[256,512]{1,0:T(8,128)(2,1)S(1)}, bf16[256,512]{1,0:T(8,128)(2,1)S(1)}, u32[]{:S(2)}, u32[]{:S(2)}) collective-permute-start(bf16[256,512]{1,0:T(8,128)(2,1)S(1)} %get-tuple-element.22), channel_id=1, source_target_pairs={{2,9},{4,11},{6,13},{9,2},{10,17},{11,4},{12,19},{13,6},{14,21},{1... | collective-permute-start | bytes 786440 | tf_op jit(solution)/shard_map/ppermute | solution.py:45
  38.2 0.0 copy-done.3
  38.2 10.4 %shard_map.97 = bf16[1,2,512,256]{3,2,1,0:T(8,128)(2,1)} custom-call(f32[2,256,256]{2,1,0:T(8,128)S(1)} %get-tuple-element.23.gram, bf16[1,2,512,256]{3,2,1,0:T(8,128)(2,1)S(1)} %copy-done.3), custom_call_target="tpu_custom_call" | custom-call | flops 12000000000 | bytes 4194304 | tf_op jit(solution)/shard_map/pallas_call | solution.py:377
  48.7 0.0 collective-permute-done.5.ne_b
  48.7 7.4 %collective-permute-start.10 = (f32[256,256]{1,0:T(8,128)S(1)}, f32[256,256]{1,0:T(8,128)S(1)}, u32[]{:S(2)}, u32[]{:S(2)}) collective-permute-start(f32[256,256]{1,0:T(8,128)S(1)} %add.3.own), channel_id=1, source_target_pairs={{0,1},{1,0},{2,3},{3,2},{4,5},{5,4},{6,7},{7,6},{8,9},{9,8},{10,11... | collective-permute-start | bytes 786440 | tf_op jit(solution)/shard_map/ppermute | solution.py:45
  56.1 0.0 collective-permute-done.6.nw_a
  56.1 0.0 collective-permute-done.7.nw_b
  56.1 0.0 collective-permute-done.gx_a
  56.1 0.0 collective-permute-done.1.gx_b
  56.1 5.4 %shard_map.95 = bf16[1,2,512,256]{3,2,1,0:T(8,128)(2,1)} custom-call(s32[1,2,5]{2,1,0:T(2,128)S(1)} %copy-done.5, f32[1,2,5,512]{3,2,1,0:T(8,128)S(1)} %copy.11.scales, bf16[1,2,5,512,512]{4,3,2,1,0:T(8,128)(2,1)} %tiles.3, f32[2,256,512]{2,1,0:T(8,128)S(1)} %get-tuple-element.14.acc, bf16[3,256,512]{2,1,0:T(8,128)(2,1)S(1)} %collective-permute-done.gx_a, ...), custom_call_target="tpu_custom_call" | custom-call | flops 3000000000 | bytes 10485760 | tf_op jit(solution)/shard_map/pallas_call | solution.py:390
  61.5 0.5 collective-permute-done.10.other
  62.0 7.5 %shard_map.99 = f32[1,1,256,256]{3,2,1,0:T(8,128)} custom-call(f32[256,256]{1,0:T(8,128)S(1)} %add.3.own, f32[256,256]{1,0:T(8,128)S(1)} %collective-permute-done.10.other), custom_call_target="tpu_custom_call" | custom-call | flops 8000000000 | bytes 1048576 | tf_op jit(solution)/shard_map/pallas_call | solution.py:387
  (1 shorter events, 0.0 us)
Async XLA Ops:
  0.6 1.0 %copy-start = (f32[1,2,256,256]{3,2,1,0:T(8,128)S(1)}, f32[1,2,256,256]{3,2,1,0:T(8,128)}, u32[]{:S(2)}) copy-start(f32[1,2,256,256]{3,2,1,0:T(8,128)} %transfer.1) | copy-start | bytes 1572868
  1.7 1.0 %copy-start.2 = (bf16[1,2,512,256]{3,2,1,0:T(8,128)(2,1)S(1)}, bf16[1,2,512,256]{3,2,1,0:T(8,128)(2,1)}, u32[]{:S(2)}) copy-start(bf16[1,2,512,256]{3,2,1,0:T(8,128)(2,1)} %basis.3) | copy-start | bytes 1572868
  2.7 0.9 %copy-start.4 = (f32[1,1,128,256]{3,2,1,0:T(8,128)S(1)}, f32[1,1,128,256]{3,2,1,0:T(8,128)}, u32[]{:S(2)}) copy-start(f32[1,1,128,256]{3,2,1,0:T(8,128)} %node.1) | copy-start | bytes 393220
  5.8 18.8 %collective-permute-start.8 = (f32[384,256]{1,0:T(8,128)S(1)}, f32[384,256]{1,0:T(8,128)S(1)}, u32[]{:S(2)}, u32[]{:S(2)}) collective-permute-start(f32[384,256]{1,0:T(8,128)S(1)} %get-tuple-element.24.own), channel_id=1, source_target_pairs={{0,8},{1,9},{2,10},{3,11},{4,12},{5,13},{6,14},{7,15},{8,0},{9,1},... | collective-permute-start | bytes 1179656 | tf_op jit(solution)/shard_map/ppermute | solution.py:45
  7.3 1.0 %copy-start.1 = (bf16[1,2,512,256]{3,2,1,0:T(8,128)(2,1)S(1)}, bf16[1,2,512,256]{3,2,1,0:T(8,128)(2,1)}, u32[]{:S(2)}) copy-start(bf16[1,2,512,256]{3,2,1,0:T(8,128)(2,1)} %points.1) | copy-start | bytes 1572868
  8.3 0.7 copy-start.5
  9.0 29.2 %copy-start.3 = (bf16[1,2,512,256]{3,2,1,0:T(8,128)(2,1)S(1)}, bf16[1,2,512,256]{3,2,1,0:T(8,128)(2,1)}, u32[]{:S(2)}) copy-start(bf16[1,2,512,256]{3,2,1,0:T(8,128)(2,1)} %basis.3) | copy-start | bytes 1572868
  14.3 12.8 %collective-permute-start.2 = (bf16[256,512]{1,0:T(8,128)(2,1)S(1)}, bf16[256,512]{1,0:T(8,128)(2,1)S(1)}, u32[]{:S(2)}, u32[]{:S(2)}) collective-permute-start(bf16[256,512]{1,0:T(8,128)(2,1)S(1)} %get-tuple-element.17), channel_id=1, source_target_pairs={{0,1},{1,0},{2,3},{3,2},{4,5},{5,4},{6,7},{7,6},{8,9},{9,8},{10,11... | collective-permute-start | bytes 786440 | tf_op jit(solution)/shard_map/ppermute | solution.py:45
  16.0 13.6 %collective-permute-start.3 = (bf16[256,512]{1,0:T(8,128)(2,1)S(1)}, bf16[256,512]{1,0:T(8,128)(2,1)S(1)}, u32[]{:S(2)}, u32[]{:S(2)}) collective-permute-start(bf16[256,512]{1,0:T(8,128)(2,1)S(1)} %get-tuple-element.18), channel_id=1, source_target_pairs={{1,2},{2,1},{3,4},{4,3},{5,6},{6,5},{9,10},{10,9},{11,12},{12,11},... | collective-permute-start | bytes 786440 | tf_op jit(solution)/shard_map/ppermute | solution.py:45
  16.7 14.1 %collective-permute-start.4 = (bf16[256,512]{1,0:T(8,128)(2,1)S(1)}, bf16[256,512]{1,0:T(8,128)(2,1)S(1)}, u32[]{:S(2)}, u32[]{:S(2)}) collective-permute-start(bf16[256,512]{1,0:T(8,128)(2,1)S(1)} %get-tuple-element.19), channel_id=1, source_target_pairs={{0,9},{2,11},{4,13},{6,15},{8,17},{9,0},{10,19},{11,2},{12,21},{13... | collective-permute-start | bytes 786440 | tf_op jit(solution)/shard_map/ppermute | solution.py:45
  25.7 11.6 %collective-permute-start.9 = (f32[256,256]{1,0:T(8,128)S(1)}, f32[256,256]{1,0:T(8,128)S(1)}, u32[]{:S(2)}, u32[]{:S(2)}) collective-permute-start(f32[256,256]{1,0:T(8,128)S(1)} %shard_map.98), channel_id=1, source_target_pairs={{0,16},{1,17},{2,18},{3,19},{4,20},{5,21},{6,22},{7,23},{8,24},{9,... | collective-permute-start | bytes 786440 | tf_op jit(solution)/shard_map/ppermute | solution.py:45
  27.1 29.0 %collective-permute-start = (bf16[3,256,512]{2,1,0:T(8,128)(2,1)S(1)}, bf16[3,256,512]{2,1,0:T(8,128)(2,1)S(1)}, u32[]{:S(2)}, u32[]{:S(2)}) collective-permute-start(bf16[3,256,512]{2,1,0:T(8,128)(2,1)S(1)} %get-tuple-element.15), channel_id=1, source_target_pairs={{0,8},{1,9},{2,10},{3,11},{4,12},{5,13},{6,14},{7,15},{8,0},{9,1},... | collective-permute-start | bytes 2359304 | tf_op jit(solution)/shard_map/ppermute | solution.py:45
  27.1 29.0 %collective-permute-start.1 = (bf16[3,256,512]{2,1,0:T(8,128)(2,1)S(1)}, bf16[3,256,512]{2,1,0:T(8,128)(2,1)S(1)}, u32[]{:S(2)}, u32[]{:S(2)}) collective-permute-start(bf16[3,256,512]{2,1,0:T(8,128)(2,1)S(1)} %get-tuple-element.16), channel_id=1, source_target_pairs={{8,16},{9,17},{10,18},{11,19},{12,20},{13,21},{14,22},{15,23},{16,... | collective-permute-start | bytes 2359304 | tf_op jit(solution)/shard_map/ppermute | solution.py:45
  29.6 19.1 %collective-permute-start.5 = (bf16[256,512]{1,0:T(8,128)(2,1)S(1)}, bf16[256,512]{1,0:T(8,128)(2,1)S(1)}, u32[]{:S(2)}, u32[]{:S(2)}) collective-permute-start(bf16[256,512]{1,0:T(8,128)(2,1)S(1)} %get-tuple-element.20), channel_id=1, source_target_pairs={{1,10},{3,12},{5,14},{9,18},{10,1},{11,20},{12,3},{13,22},{14,5},{... | collective-permute-start | bytes 786440 | tf_op jit(solution)/shard_map/ppermute | solution.py:45
  30.8 25.3 %collective-permute-start.6 = (bf16[256,512]{1,0:T(8,128)(2,1)S(1)}, bf16[256,512]{1,0:T(8,128)(2,1)S(1)}, u32[]{:S(2)}, u32[]{:S(2)}) collective-permute-start(bf16[256,512]{1,0:T(8,128)(2,1)S(1)} %get-tuple-element.21), channel_id=1, source_target_pairs={{1,8},{3,10},{5,12},{7,14},{8,1},{9,16},{10,3},{11,18},{12,5},{13,... | collective-permute-start | bytes 786440 | tf_op jit(solution)/shard_map/ppermute | solution.py:45
  37.3 18.8 %collective-permute-start.7 = (bf16[256,512]{1,0:T(8,128)(2,1)S(1)}, bf16[256,512]{1,0:T(8,128)(2,1)S(1)}, u32[]{:S(2)}, u32[]{:S(2)}) collective-permute-start(bf16[256,512]{1,0:T(8,128)(2,1)S(1)} %get-tuple-element.22), channel_id=1, source_target_pairs={{2,9},{4,11},{6,13},{9,2},{10,17},{11,4},{12,19},{13,6},{14,21},{1... | collective-permute-start | bytes 786440 | tf_op jit(solution)/shard_map/ppermute | solution.py:45
  48.7 13.3 %collective-permute-start.10 = (f32[256,256]{1,0:T(8,128)S(1)}, f32[256,256]{1,0:T(8,128)S(1)}, u32[]{:S(2)}, u32[]{:S(2)}) collective-permute-start(f32[256,256]{1,0:T(8,128)S(1)} %add.3.own), channel_id=1, source_target_pairs={{0,1},{1,0},{2,3},{3,2},{4,5},{5,4},{6,7},{7,6},{8,9},{9,8},{10,11... | collective-permute-start | bytes 786440 | tf_op jit(solution)/shard_map/ppermute | solution.py:45
where the time goes:
time: 70 us; the launch traced here: 69.5 us
  Pallas kernels  31.9 us (46%)
  starting transfers between devices  30.4 us (43%)
  local copies, waits for them, and re-layouts  5.43 us (8%)
  waiting for transfers between devices  0.99 us (1%)
  between operations  0.79 us (1%)
    ppermute x11, starting transfers between devices, swap(): return lax.ppermute(block, axes, route)  30.4 us
    pallas_call x1, Pallas kernels, shards(): call(leaf_kernel, shape(*basis.shape), [VMEM] * 2, VMEM, [pltpu.VMEM((2,...  10.4 us
    pallas_call x1, Pallas kernels, shards(): call(top_kernel, shape(1, 1, rank, rank, dtype=F32), [VMEM] * 2, VMEM, fl...  7.49 us
    unnamed x13, local copies, waits for them, and re-layouts  5.43 us
    pallas_call x1, Pallas kernels, shards(): call(near_kernel, shape(*points_x.shape), [SMEM, VMEM, ANY, VMEM, *[ANY]...  5.39 us
    pallas_call x1, Pallas kernels, shards(): call(mirror_kernel, (shape(2, vecs, pts, dtype=F32), trio, trio, *[block]...  5.26 us
    pallas_call x1, Pallas kernels, shards(): call(gram_kernel, (shape(2, rank, rank, dtype=F32), shape(rank + half, ra...  2.17 us
  transfers between devices with their start and end apart: 11, of which 2 were waited for; matrix products, arithmetic and copies ran while one was open for 1% of the time, Pallas kernels for 32%

commit v1 on v0

v1 whole, which is shorter than its diff:
```python
import jax
import jax.numpy as jnp
from jax import lax
from jax.experimental import pallas as pl
from jax.experimental.pallas import tpu as pltpu
from jax.sharding import PartitionSpec as P

F32 = jnp.float32
BF16 = jnp.bfloat16
ANY = pl.BlockSpec(memory_space=pl.ANY)
VMEM = pl.BlockSpec(memory_space=pltpu.VMEM)
SMEM = pl.BlockSpec(memory_space=pltpu.SMEM)
PANEL = 32
PIECE = 16


def dot(a, b, dims, precision=lax.Precision.HIGHEST):
    return lax.dot_general(a, b, (dims, ((), ())), precision=precision, preferred_element_type=F32)


def nn(a, b):
    return dot(a, b, ((1,), (0,)))


def tn(a, b):
    return dot(a, b, ((0,), (0,)))


def bf_nn(a, b):
    return dot(a, b, ((1,), (0,)), lax.Precision.DEFAULT)


def bf_nt(a, b):
    return dot(a, b, ((1,), (1,)), lax.Precision.DEFAULT)


def send(block, axes, sizes, partner):
    count_x, count_y = sizes
    route = []
    for i in range(count_x):
        for j in range(count_y):
            x, y = partner(i, j)
            route.append((i * count_y + j, x % count_x * count_y + y % count_y))
    return lax.ppermute(block, axes, route)


def panel_step(k, tiles, nb, sb):
    iota = lax.broadcasted_iota(jnp.int32, (8, 128), 0)
    groups = nb // 8
    scale = [jnp.ones((8, 128), F32) for _ in range(groups)]
    for s in range(0, nb, sb):
        base = (k + s) % 128
        g0 = s // 8
        cols = []
        for j in range(sb):
            cols.append(
                {
                    g: jnp.broadcast_to(tiles[g][0][:, base + j : base + j + 1], (8, 128))
                    for g in range(g0 + j // 8, groups)
                }
            )
        for p in range(sb):
            gp = g0 + p // 8
            r = p % 8
            pivot = jnp.broadcast_to(cols[p][gp][r : r + 1, :], (8, 128))
            inv = 1.0 / pivot
            scale[gp] = jnp.where(iota == r, lax.rsqrt(pivot), scale[gp])
            for j in range(p + 1, sb):
                gj = g0 + j // 8
                t = jnp.broadcast_to(cols[p][gj][j % 8 : j % 8 + 1, :], (8, 128)) * inv
                for g in range(gj, groups):
                    cols[j][g] = cols[j][g] - cols[p][g] * t
            rows = [jnp.broadcast_to(t[r : r + 1, :], (8, 128)) * inv for t in tiles[gp]]
            for g in range(gp, groups):
                c = cols[p][g]
                if g == gp:
                    if r == 7:
                        continue
                    c = jnp.where(iota > r, c, 0.0)
                tiles[g] = [t - c * w for t, w in zip(tiles[g], rows)]
    return [[t * scale[g] for t in tiles[g]] for g in range(groups)]


def factorize(reads, u_refs, w_refs, n):
    lanes = lax.broadcasted_iota(jnp.int32, (8, 128), 1)
    sub = lax.broadcasted_iota(jnp.int32, (8, 128), 0)
    nb = PANEL
    for k in range(0, n, nb):
        lo = k // 128 * 128
        hi = (k + nb - 1) // 128 * 128 + 128
        for read, u, w in zip(reads, u_refs, w_refs):
            main = read(slice(k, k + nb), slice(lo, n))
            side = jnp.zeros((nb, hi), F32)
            if k:
                col = u[0:k, k : k + nb]
                main = main - tn(col, u[0:k, lo:n])
                if w is not None:
                    side = -tn(col, w[0:k, 0:hi])
            tiles = []
            for g in range(nb // 8):
                row = [main[8 * g : 8 * g + 8, c : c + 128] for c in range(0, n - lo, 128)]
                if w is not None:
                    more = [side[8 * g : 8 * g + 8, c : c + 128] for c in range(0, hi, 128)]
                    more[-1] = more[-1] + jnp.where(lanes == sub + (k + 8 * g - (hi - 128)), 1.0, 0.0)
                    row += more
                tiles.append(row)
            tiles = panel_step(k, tiles, nb, PIECE)
            na = (n - lo) // 128
            for g in range(nb // 8):
                first = k + 8 * g
                r = slice(first, first + 8)
                for i in range(na):
                    c = lo + 128 * i
                    t = tiles[g][i]
                    if c == lo:
                        t = jnp.where(lanes + c >= sub + first, t, 0.0)
                    u[r, c : c + 128] = t
                for c in range(0, lo, 128):
                    u[r, c : c + 128] = jnp.zeros((8, 128), F32)
                if w is not None:
                    for i, c in enumerate(range(0, hi, 128)):
                        w[r, c : c + 128] = tiles[g][na + i]
                    for c in range(hi, n, 128):
                        w[r, c : c + 128] = jnp.zeros((8, 128), F32)


def node_kernel(own, other, out, stacked):
    rank = own.shape[1]
    half = rank // 2
    parity = lax.axis_index("gx") % 2
    gram = 0.25 * (own[0:rank, :] + other[0:rank, :])
    mine = pl.multiple_of(parity * half, half)
    theirs = pl.multiple_of((1 - parity) * half, half)
    stacked[pl.ds(mine, half), :] = own[rank : rank + half, :]
    stacked[pl.ds(theirs, half), :] = other[rank : rank + half, :]
    t = stacked[...]
    out[...] = 0.25 * tn(t, nn(gram, t))


def leaf_kernel(gram, basis, q, u, w):
    n = gram.shape[1]
    reads = [lambda r, c, m=m: gram[m, r, c] for m in range(2)]
    factorize(reads, [u.at[m] for m in range(2)], [w.at[m] for m in range(2)], n)
    for leaf in range(2):
        rest = w[leaf]
        total = None
        for _ in range(3):
            part = rest.astype(BF16)
            rest = rest - part.astype(F32)
            term = bf_nt(basis[0, leaf], part)
            total = term if total is None else total + term
        q[0, leaf] = total.astype(BF16)


def top_kernel(own, other, out):
    n = own.shape[0]
    factorize([lambda r, c: own[r, c] + other[r, c]], [out.at[0, 0]], [None], n)


def slot_of(slots, leaf, direction):
    found = 0
    for s in range(5):
        found = found + jnp.where(slots[0, leaf, s] == direction, s, 0)
    return found


def first_kernel(basis_h, transfer_h, node_h, slots_h, points_h, scales_h, tiles_h,
                 gram_h, sent_h, low_h, high_h, up_h, x_h, gx_a, gx_b,
                 gram, sent, acc, basis, transfer, slots, points, scales, tiles, east, west, in_sems, tile_sems, out_sems):
    rank = gram.shape[1]
    half = node_h.shape[2]
    sources = (
        (basis_h, basis), (transfer_h, transfer), (slots_h, slots), (points_h, points), (scales_h, scales),
        (node_h.at[0, 0], sent.at[pl.ds(rank, half)]),
    )
    loads = [pltpu.make_async_copy(a, b, in_sems.at[i]) for i, (a, b) in enumerate(sources)]
    for load in loads:
        load.start()

    def tile_copy(leaf, slot):
        return pltpu.make_async_copy(tiles_h.at[0, leaf, slot], tiles.at[leaf, slot], tile_sems.at[leaf, slot])

    for leaf in range(2):
        for slot in range(5):
            tile_copy(leaf, slot).start()

    loads[0].wait()
    loads[1].wait()
    total = None
    for leaf in range(2):
        b = basis[0, leaf]
        g = dot(b, b, ((0,), (0,)), lax.Precision.DEFAULT) / basis.shape[2]
        gram[leaf] = g
        t = transfer[0, leaf]
        part = tn(t, nn(g, t))
        total = part if total is None else total + part
    sent[0:rank, :] = total
    for load in loads[2:]:
        load.wait()
    waits = []

    def store(scratch, target):
        waits.append(pltpu.make_async_copy(scratch, target, out_sems.at[len(waits)]))
        waits[-1].start()

    store(gram, gram_h)
    store(sent, sent_h)
    west[0] = points[0, 0].T
    west[3] = points[0, 1].T
    east[3] = west[3]
    xt = (west.at[0], west.at[3])
    store(west.at[0], x_h)
    for leaf in range(2):
        for slot in range(5):
            tile_copy(leaf, slot).wait()

    def mirrored(leaf, d):
        slot = slot_of(slots, leaf, d)
        scaled = (xt[leaf][...].astype(F32) * scales[0, slot, pl.ds(leaf, 1), :]).astype(BF16)
        return bf_nn(scaled, tiles[leaf, slot])

    def direct(leaf, d, x):
        slot = slot_of(slots, leaf, d)
        return bf_nt(x, tiles[leaf, slot]) * scales[0, slot, pl.ds(leaf, 1), :]

    east[0] = mirrored(0, 1).astype(BF16)
    west[1] = mirrored(0, 4).astype(BF16)
    east[1] = (mirrored(0, 3) + mirrored(1, 1)).astype(BF16)
    east[2] = mirrored(1, 3).astype(BF16)
    west[2] = mirrored(1, 4).astype(BF16)
    even = lax.axis_index("gx") % 2 == 0

    @pl.when(even)
    def _():
        pltpu.make_async_copy(east, gx_a, out_sems.at[3]).start()
        pltpu.make_async_copy(west, gx_b, out_sems.at[4]).start()

    @pl.when(jnp.logical_not(even))
    def _():
        pltpu.make_async_copy(west, gx_a, out_sems.at[3]).start()
        pltpu.make_async_copy(east, gx_b, out_sems.at[4]).start()

    waits.append(pltpu.make_async_copy(east, gx_a, out_sems.at[3]))
    waits.append(pltpu.make_async_copy(west, gx_b, out_sems.at[4]))
    acc[0] = mirrored(1, 2)
    store(acc.at[0], up_h)
    acc[1] = direct(0, 0, xt[0][...]) + direct(0, 2, xt[1][...])
    store(acc.at[1], low_h)
    acc[2] = direct(1, 0, xt[1][...]) + mirrored(0, 2)
    store(acc.at[2], high_h)
    for w in waits:
        w.wait()


def sides():
    gx, gy = lax.axis_index("gx"), lax.axis_index("gy")
    last_x, last_y = lax.axis_size("gx") - 1, lax.axis_size("gy") - 1
    return gx < last_x, gx > 0, gy < last_y, gy > 0, gx % 2 == 0


def kept(inside, product):
    return jnp.where(inside, product.astype(F32), 0.0)


def up_kernel(own, a, b, out):
    east, west, _, _, even = sides()
    out[...] = (own[...] + a[2].astype(F32) + kept(jnp.where(even, west, east), b[2])).astype(BF16)


def near_kernel(slots, scales, tiles_h, low_in, high_in, gx_a, gx_b, n, ne, nw, out, low_out, tiles, done, sems, done_sem):
    order = ((0, 1), (0, 3), (0, 4), (1, 1), (1, 2), (1, 3), (1, 4))

    def tile_copy(leaf, d):
        place = order.index((leaf, d))
        return pltpu.make_async_copy(tiles_h.at[0, leaf, slot_of(slots, leaf, d)], tiles.at[place], sems.at[place])

    for leaf, d in order:
        tile_copy(leaf, d).start()
    east, west, north, _, even = sides()
    beside = jnp.where(even, west, east)

    def from_east(i):
        return jnp.where(even, gx_a[i], gx_b[i])

    def from_west(i):
        return jnp.where(even, gx_b[i], gx_a[i])

    def direct(leaf, d, x, inside):
        tile_copy(leaf, d).wait()
        scale = jnp.where(inside, scales[0, slot_of(slots, leaf, d), pl.ds(leaf, 1), :], 0.0)
        return bf_nt(x, tiles[order.index((leaf, d))]) * scale

    x1_east = from_east(3)
    low = low_in[...] + kept(west, from_west(0)) + direct(0, 1, from_east(0), east)
    low = low + direct(0, 3, x1_east, east)
    low_out[...] = low + direct(0, 4, from_west(3), west)
    high = high_in[...] + gx_a[1].astype(F32) + kept(beside, gx_b[1]) + direct(1, 1, x1_east, east)
    high = high + direct(1, 2, n[...], north)
    high = high + direct(1, 3, ne[...], north & east)
    high = high + direct(1, 4, nw[...], north & west)
    done[...] = high.T.astype(BF16)
    copy = pltpu.make_async_copy(done, out.at[0, 1], done_sem)
    copy.start()
    copy.wait()


def last_kernel(near, low, south, out, done, sem):
    _, _, _, inside, _ = sides()
    done[...] = (low[...] + kept(inside, south[...])).T.astype(BF16)
    copy = pltpu.make_async_copy(done, out.at[0, 0], sem)
    copy.start()
    copy.wait()


def shape(*dims, dtype=BF16):
    return jax.ShapeDtypeStruct(dims, dtype)


def call(kernel, outs, in_specs, out_specs, scratch=(), flops=0, moved=0, vmem=48 << 20, aliases=None):
    return pl.pallas_call(
        kernel,
        out_shape=outs,
        in_specs=in_specs,
        out_specs=out_specs,
        scratch_shapes=list(scratch),
        input_output_aliases=aliases or {},
        compiler_params=pltpu.CompilerParams(vmem_limit_bytes=vmem),
        cost_estimate=pl.CostEstimate(flops=flops, bytes_accessed=moved, transcendentals=0),
    )


def make_shards(sizes):
    axes = ("gx", "gy")

    def shards(points_x, near_tiles, scales, slot_direction, basis, leaf_transfer, node_transfer):
        pts, vecs = points_x.shape[2:]
        rank = basis.shape[3]
        half = node_transfer.shape[2]
        dma = pltpu.SemaphoreType.DMA

        block = shape(vecs, pts)
        wide = shape(vecs, pts, dtype=F32)
        sides_sent = shape(4, vecs, pts)
        scales = jnp.transpose(scales, (0, 2, 1, 3))
        gram, sent, low, high, up, own_x, gx_a, gx_b = call(
            first_kernel,
            (
                shape(2, rank, rank, dtype=F32),
                shape(rank + half, rank, dtype=F32),
                wide, wide, wide, block, sides_sent, sides_sent,
            ),
            [ANY] * 7,
            (ANY,) * 8,
            [
                pltpu.VMEM((2, rank, rank), F32),
                pltpu.VMEM((rank + half, rank), F32),
                pltpu.VMEM((3, vecs, pts), F32),
                pltpu.VMEM(basis.shape, BF16),
                pltpu.VMEM(leaf_transfer.shape, F32),
                pltpu.SMEM(slot_direction.shape, jnp.int32),
                pltpu.VMEM(points_x.shape, BF16),
                pltpu.VMEM(scales.shape, F32),
                pltpu.VMEM(near_tiles.shape[1:], BF16),
                *[pltpu.VMEM((4, vecs, pts), BF16)] * 2,
                dma((6,)),
                dma((2, 5)),
                dma((8,)),
            ],
            flops=10**6,
            moved=1 << 10,
            vmem=32 << 20,
        )(*(pltpu.with_memory_space_constraint(a, pltpu.HBM) for a in (
            basis, leaf_transfer, node_transfer, slot_direction, points_x, scales, near_tiles)))
        got = send(sent, axes, sizes, lambda i, j: (i ^ 1, j))

        got_a = send(gx_a, axes, sizes, lambda i, j: (i ^ 1, j))
        got, got_a = lax.optimization_barrier((got, got_a))
        node = call(node_kernel, shape(rank, rank, dtype=F32), [VMEM] * 2, VMEM,
                    [pltpu.VMEM((rank, rank), F32)], flops=10**6, moved=1 << 10)(sent, got)
        node_got = send(node, axes, sizes, lambda i, j: (i ^ 2, j))
        got_b = send(gx_b, axes, sizes, lambda i, j: (i - 1 if i % 2 == 0 else i + 1, j))
        n = send(own_x, axes, sizes, lambda i, j: (i, j - 1))
        ne = send(own_x, axes, sizes, lambda i, j: (i - 1, j - 1))
        nw = send(own_x, axes, sizes, lambda i, j: (i + 1, j - 1))
        leaf_q = call(
            leaf_kernel,
            shape(*basis.shape),
            [VMEM] * 2,
            VMEM,
            [pltpu.VMEM((2, rank, rank), F32), pltpu.VMEM((2, rank, rank), F32)],
            flops=10**6,
            moved=1 << 10,
        )(gram, basis)

        leaf_q, node_got, got_b = lax.optimization_barrier((leaf_q, node_got, got_b))
        pair = node + node_got
        other = send(pair, axes, sizes, lambda i, j: (i, j ^ 1))
        total_up = call(up_kernel, block, [VMEM] * 3, VMEM, moved=1 << 10)(up, got_a, got_b)
        south = send(total_up, axes, sizes, lambda i, j: (i, j + 1))

        near, low = call(
            near_kernel,
            (shape(*points_x.shape), wide),
            [SMEM, VMEM, ANY, *[VMEM] * 7],
            (ANY, VMEM),
            [pltpu.VMEM((7, pts, pts), BF16), pltpu.VMEM((pts, vecs), BF16), dma((7,)), dma],
            flops=10**6,
            moved=1 << 10,
        )(slot_direction, scales, near_tiles, low, high, got_a, got_b, n, ne, nw)
        low, other = lax.optimization_barrier((low, other))
        top = call(top_kernel, shape(1, 1, rank, rank, dtype=F32), [VMEM] * 2, VMEM, flops=10**6,
                   moved=1 << 10)(pair, other)

        near = call(
            last_kernel,
            shape(*points_x.shape),
            [ANY, VMEM, VMEM],
            ANY,
            [pltpu.VMEM((pts, vecs), BF16), dma],
            moved=1 << 10,
            aliases={0: 0},
        )(near, low, south)
        return near, leaf_q, top

    return shards


def solution(mesh):
    leaf = P("gx", "gy", None, None)
    placed = (leaf, P("gx", "gy", None, None, None), leaf, P("gx", "gy", None), leaf, leaf, leaf)
    return jax.shard_map(
        make_shards((mesh.shape["gx"], mesh.shape["gy"])),
        mesh=mesh,
        in_specs=placed,
        out_specs=(leaf, leaf, leaf),
        check_vma=False,
    )
```

time: 70 us -> 53.6 us (0.77)
  the two profiles are of different devices: /device:TPU:7 before, /device:TPU:1 now
where the time goes in v1:
time: 53.6 us; the launch traced here: 53.5 us
  Pallas kernels  32.6 us (61%)
  starting transfers between devices  17.2 us (32%)
  waiting for transfers between devices  2.81 us (5%)
  between operations  0.89 us (2%)
    ppermute x9, starting transfers between devices, send(): return lax.ppermute(block, axes, route)  17.2 us
    pallas_call x1, Pallas kernels, shards(): call(leaf_kernel, shape(*basis.shape), [VMEM] * 2, VMEM, [pltpu.VMEM((2,...  10.4 us
    pallas_call x1, Pallas kernels, shards(): call(first_kernel, (shape(2, rank, rank, dtype=F32), shape(rank + half, r...  7.61 us
    pallas_call x1, Pallas kernels, shards(): call(top_kernel, shape(1, 1, rank, rank, dtype=F32), [VMEM] * 2, VMEM, fl...  7.49 us
    pallas_call x1, Pallas kernels, shards(): call(near_kernel, (shape(*points_x.shape), wide), [SMEM, VMEM, ANY, *[VME...  4.99 us
    ppermute x9, waiting for transfers between devices, send(): return lax.ppermute(block, axes, route)  2.81 us
    pallas_call x1, Pallas kernels, shards(): call(node_kernel, shape(rank, rank, dtype=F32), [VMEM] * 2, VMEM, [pltpu....  1.12 us
  transfers between devices with their start and end apart: 9, of which 2 were waited for; matrix products, arithmetic and copies ran while one was open for 0% of the time, Pallas kernels for 45%

profile of v1, /device:TPU:1, one launch (start us, length us, event | category | flops | bytes accessed | tf_op | source)
XLA Modules:
  0.0 53.5 jit_solution(9586289298046001275)
XLA Ops:
  0.6 0.0 copy-start
  0.6 0.0 copy-start.1
  0.7 0.0 copy-start.2
  0.7 7.6 %shard_map.94 = (f32[2,256,256]{2,1,0:T(8,128)S(1)}, f32[384,256]{1,0:T(8,128)S(1)}, f32[256,512]{1,0:T(8,128)S(1)}, f32[256,512]{1,0:T(8,128)S(1)}, f32[256,512...) custom-call(bf16[1,2,512,256]{3,2,1,0:T(8,128)(2,1)} %basis.1, ...), custom_call_target="tpu_custom_call" | custom-call | flops 1000000 | bytes 1024 | tf_op jit(solution)/shard_map/pallas_call | solution.py:345
  8.3 3.3 %collective-permute-start.1 = (bf16[4,256,512]{2,1,0:T(8,128)(2,1)S(1)}, bf16[4,256,512]{2,1,0:T(8,128)(2,1)S(1)}, u32[]{:S(2)}, u32[]{:S(2)}) collective-permute-start(bf16[4,256,512]{2,1,0:T(8,128)(2,1)S(1)} %get-tuple-element.23), channel_id=1, source_target_pairs={{0,8},{1,9},{2,10},{3,11},{4,12},{5,13},{6,14},{7,15},{8,0},{9,1},... | collective-permute-start | bytes 3145736 | tf_op jit(solution)/shard_map/ppermute | solution.py:44
  11.6 0.0 collective-permute-start.3
  11.6 3.6 %collective-permute-start = (f32[384,256]{1,0:T(8,128)S(1)}, f32[384,256]{1,0:T(8,128)S(1)}, u32[]{:S(2)}, u32[]{:S(2)}) collective-permute-start(f32[384,256]{1,0:T(8,128)S(1)} %get-tuple-element.22.own), channel_id=1, source_target_pairs={{0,8},{1,9},{2,10},{3,11},{4,12},{5,13},{6,14},{7,15},{8,0},{9,1},... | collective-permute-start | bytes 1179656 | tf_op jit(solution)/shard_map/ppermute | solution.py:44
  15.2 1.3 %collective-permute-done.other = f32[384,256]{1,0:T(8,128)S(1)} collective-permute-done((f32[384,256]{1,0:T(8,128)S(1)}, f32[384,256]{1,0:T(8,128)S(1)}, u32[]{:S(2)}, u32[]{:S(2)}) %collective-permute-start) | collective-permute-done | bytes 393248 | tf_op jit(solution)/shard_map/ppermute | solution.py:44
  16.6 0.0 collective-permute-done.1.gx_a.a
  16.6 1.1 %shard_map.96 = f32[256,256]{1,0:T(8,128)S(1)} custom-call(f32[384,256]{1,0:T(8,128)S(1)} %get-tuple-element.22.own, f32[384,256]{1,0:T(8,128)S(1)} %collective-permute-done.other), custom_call_target="tpu_custom_call" | custom-call | flops 1000000 | bytes 1024 | tf_op jit(solution)/shard_map/pallas_call | solution.py:378
  17.7 0.1 collective-permute-start.2
  17.8 5.7 %collective-permute-start.4 = (bf16[256,512]{1,0:T(8,128)(2,1)S(1)}, bf16[256,512]{1,0:T(8,128)(2,1)S(1)}, u32[]{:S(2)}, u32[]{:S(2)}) collective-permute-start(bf16[256,512]{1,0:T(8,128)(2,1)S(1)} %get-tuple-element.29), channel_id=1, source_target_pairs={{0,7},{1,0},{2,1},{3,2},{4,3},{5,4},{6,5},{7,6},{8,15},{9,8},{10,9... | collective-permute-start | bytes 786440 | tf_op jit(solution)/shard_map/ppermute | solution.py:44
  23.4 1.3 %collective-permute-start.5 = (bf16[256,512]{1,0:T(8,128)(2,1)S(1)}, bf16[256,512]{1,0:T(8,128)(2,1)S(1)}, u32[]{:S(2)}, u32[]{:S(2)}) collective-permute-start(bf16[256,512]{1,0:T(8,128)(2,1)S(1)} %get-tuple-element.29), channel_id=1, source_target_pairs={{0,255},{1,248},{2,249},{3,250},{4,251},{5,252},{6,253},{7,254},{8... | collective-permute-start | bytes 786440 | tf_op jit(solution)/shard_map/ppermute | solution.py:44
  24.7 1.4 %collective-permute-start.6 = (bf16[256,512]{1,0:T(8,128)(2,1)S(1)}, bf16[256,512]{1,0:T(8,128)(2,1)S(1)}, u32[]{:S(2)}, u32[]{:S(2)}) collective-permute-start(bf16[256,512]{1,0:T(8,128)(2,1)S(1)} %get-tuple-element.29), channel_id=1, source_target_pairs={{0,15},{1,8},{2,9},{3,10},{4,11},{5,12},{6,13},{7,14},{8,23},{9,16... | collective-permute-start | bytes 786440 | tf_op jit(solution)/shard_map/ppermute | solution.py:44
  26.1 0.0 copy-done
  26.1 10.4 %shard_map.95 = bf16[1,2,512,256]{3,2,1,0:T(8,128)(2,1)} custom-call(f32[2,256,256]{2,1,0:T(8,128)S(1)} %get-tuple-element.25.gram, bf16[1,2,512,256]{3,2,1,0:T(8,128)(2,1)S(1)} %copy-done), custom_call_target="tpu_custom_call" | custom-call | flops 1000000 | bytes 1024 | tf_op jit(solution)/shard_map/pallas_call | solution.py:385
  36.5 0.0 collective-permute-done.3.gx_b.b
  36.5 0.0 collective-permute-done.2
  36.6 0.8 %collective-permute-start.7 = (f32[256,256]{1,0:T(8,128)S(1)}, f32[256,256]{1,0:T(8,128)S(1)}, u32[]{:S(2)}, u32[]{:S(2)}) collective-permute-start(f32[256,256]{1,0:T(8,128)S(1)} %add.3.own), channel_id=1, source_target_pairs={{0,1},{1,0},{2,3},{3,2},{4,5},{5,4},{6,7},{7,6},{8,9},{9,8},{10,11... | collective-permute-start | bytes 786440 | tf_op jit(solution)/shard_map/ppermute | solution.py:44
  37.4 0.1 shard_map.98
  37.5 1.0 %collective-permute-start.8 = (bf16[256,512]{1,0:T(8,128)(2,1)S(1)}, bf16[256,512]{1,0:T(8,128)(2,1)S(1)}, u32[]{:S(2)}, u32[]{:S(2)}) collective-permute-start(bf16[256,512]{1,0:T(8,128)(2,1)S(1)} %shard_map.98), channel_id=1, source_target_pairs={{0,1},{1,2},{2,3},{3,4},{4,5},{5,6},{6,7},{7,0},{8,9},{9,10},{10,1... | collective-permute-start | bytes 786440 | tf_op jit(solution)/shard_map/ppermute | solution.py:44
  38.5 0.0 collective-permute-done.4.n
  38.5 0.0 collective-permute-done.5.ne
  38.6 1.4 %collective-permute-done.6.nw = bf16[256,512]{1,0:T(8,128)(2,1)S(1)} collective-permute-done((bf16[256,512]{1,0:T(8,128)(2,1)S(1)}, bf16[256,512]{1,0:T(8,128)(2,1)S(1)}, u32[]{:S(2)}, u32[]{:S(2)}) %collective-permute-start.6) | collective-permute-done | bytes 262176 | tf_op jit(solution)/shard_map/ppermute | solution.py:44
  40.0 0.0 copy-done.1
  40.0 0.0 copy-done.2
  40.0 5.0 %shard_map.97 = (bf16[1,2,512,256]{3,2,1,0:T(8,128)(2,1)}, f32[256,512]{1,0:T(8,128)S(1)}) custom-call(s32[1,2,5]{2,1,0:T(2,128)S(1)} %copy-done.2, f32[1,5,2,512]{3,2,1,0:T(2,128)S(1)} %bitcast.2, bf16[1,2,5,512,512]{4,3,2,1,0:T(8,128)(2,1)} %tiles_h.3, f32[256,512]{1,0:T(8,128)S(1)} %get-tuple-element.20.low_in, f32[256,512]{1,0:T(8,128)S(1)} %get-tuple-element.21.high_in, ...), custom_call_target="tpu_custom_call" | custom-call | flops 1000000 | bytes 1024 | tf_op jit(solution)/shard_map/pallas_call | solution.py:401
  45.0 0.0 collective-permute-done.7.other
  45.0 7.5 %shard_map.100 = f32[1,1,256,256]{3,2,1,0:T(8,128)} custom-call(f32[256,256]{1,0:T(8,128)S(1)} %add.3.own, f32[256,256]{1,0:T(8,128)S(1)} %collective-permute-done.7.other), custom_call_target="tpu_custom_call" | custom-call | flops 1000000 | bytes 1024 | tf_op jit(solution)/shard_map/pallas_call | solution.py:411
  52.5 0.0 collective-permute-done.8.south
  52.5 0.9 %shard_map.99 = bf16[1,2,512,256]{3,2,1,0:T(8,128)(2,1)} custom-call(bf16[1,2,512,256]{3,2,1,0:T(8,128)(2,1)} %get-tuple-element.30.near, f32[256,512]{1,0:T(8,128)S(1)} %get-tuple-element.33.low, bf16[256,512]{1,0:T(8,128)(2,1)S(1)} %collective-permute-done.8.south), custom_call_target="tpu_custom_call", output_to_operand_aliasing={{}: (0, {})} | custom-call | bytes 1024 | tf_op jit(solution)/shard_map/pallas_call | solution.py:414
  (1 shorter events, 0.0 us)
Async XLA Ops:
  0.6 25.5 %copy-start = (bf16[1,2,512,256]{3,2,1,0:T(8,128)(2,1)S(1)}, bf16[1,2,512,256]{3,2,1,0:T(8,128)(2,1)}, u32[]{:S(2)}) copy-start(bf16[1,2,512,256]{3,2,1,0:T(8,128)(2,1)} %basis.1) | copy-start | bytes 1572868
  0.6 39.4 %copy-start.1 = (f32[1,2,5,512]{3,1,2,0:T(2,128)S(1)}, f32[1,2,5,512]{3,1,2,0:T(2,128)}, u32[]{:S(2)}) copy-start(f32[1,2,5,512]{3,1,2,0:T(2,128)} %param.9) | copy-start | bytes 61444
  0.7 39.3 %copy-start.2 = (s32[1,2,5]{2,1,0:T(2,128)S(1)}, s32[1,2,5]{2,1,0:T(2,128)}, u32[]{:S(2)}) copy-start(s32[1,2,5]{2,1,0:T(2,128)} %slots.1) | copy-start | bytes 124
  8.3 8.3 %collective-permute-start.1 = (bf16[4,256,512]{2,1,0:T(8,128)(2,1)S(1)}, bf16[4,256,512]{2,1,0:T(8,128)(2,1)S(1)}, u32[]{:S(2)}, u32[]{:S(2)}) collective-permute-start(bf16[4,256,512]{2,1,0:T(8,128)(2,1)S(1)} %get-tuple-element.23), channel_id=1, source_target_pairs={{0,8},{1,9},{2,10},{3,11},{4,12},{5,13},{6,14},{7,15},{8,0},{9,1},... | collective-permute-start | bytes 3145736 | tf_op jit(solution)/shard_map/ppermute | solution.py:44
  11.6 24.9 %collective-permute-start.3 = (bf16[4,256,512]{2,1,0:T(8,128)(2,1)S(1)}, bf16[4,256,512]{2,1,0:T(8,128)(2,1)S(1)}, u32[]{:S(2)}, u32[]{:S(2)}) collective-permute-start(bf16[4,256,512]{2,1,0:T(8,128)(2,1)S(1)} %get-tuple-element.27), channel_id=1, source_target_pairs={{0,248},{1,249},{2,250},{3,251},{4,252},{5,253},{6,254},{7,255},{8... | collective-permute-start | bytes 3145736 | tf_op jit(solution)/shard_map/ppermute | solution.py:44
  11.6 4.9 %collective-permute-start = (f32[384,256]{1,0:T(8,128)S(1)}, f32[384,256]{1,0:T(8,128)S(1)}, u32[]{:S(2)}, u32[]{:S(2)}) collective-permute-start(f32[384,256]{1,0:T(8,128)S(1)} %get-tuple-element.22.own), channel_id=1, source_target_pairs={{0,8},{1,9},{2,10},{3,11},{4,12},{5,13},{6,14},{7,15},{8,0},{9,1},... | collective-permute-start | bytes 1179656 | tf_op jit(solution)/shard_map/ppermute | solution.py:44
  17.7 18.8 %collective-permute-start.2 = (f32[256,256]{1,0:T(8,128)S(1)}, f32[256,256]{1,0:T(8,128)S(1)}, u32[]{:S(2)}, u32[]{:S(2)}) collective-permute-start(f32[256,256]{1,0:T(8,128)S(1)} %shard_map.96), channel_id=1, source_target_pairs={{0,16},{1,17},{2,18},{3,19},{4,20},{5,21},{6,22},{7,23},{8,24},{9,... | collective-permute-start | bytes 786440 | tf_op jit(solution)/shard_map/ppermute | solution.py:44
  17.8 20.8 %collective-permute-start.4 = (bf16[256,512]{1,0:T(8,128)(2,1)S(1)}, bf16[256,512]{1,0:T(8,128)(2,1)S(1)}, u32[]{:S(2)}, u32[]{:S(2)}) collective-permute-start(bf16[256,512]{1,0:T(8,128)(2,1)S(1)} %get-tuple-element.29), channel_id=1, source_target_pairs={{0,7},{1,0},{2,1},{3,2},{4,3},{5,4},{6,5},{7,6},{8,15},{9,8},{10,9... | collective-permute-start | bytes 786440 | tf_op jit(solution)/shard_map/ppermute | solution.py:44
  23.4 15.1 %collective-permute-start.5 = (bf16[256,512]{1,0:T(8,128)(2,1)S(1)}, bf16[256,512]{1,0:T(8,128)(2,1)S(1)}, u32[]{:S(2)}, u32[]{:S(2)}) collective-permute-start(bf16[256,512]{1,0:T(8,128)(2,1)S(1)} %get-tuple-element.29), channel_id=1, source_target_pairs={{0,255},{1,248},{2,249},{3,250},{4,251},{5,252},{6,253},{7,254},{8... | collective-permute-start | bytes 786440 | tf_op jit(solution)/shard_map/ppermute | solution.py:44
  24.7 15.3 %collective-permute-start.6 = (bf16[256,512]{1,0:T(8,128)(2,1)S(1)}, bf16[256,512]{1,0:T(8,128)(2,1)S(1)}, u32[]{:S(2)}, u32[]{:S(2)}) collective-permute-start(bf16[256,512]{1,0:T(8,128)(2,1)S(1)} %get-tuple-element.29), channel_id=1, source_target_pairs={{0,15},{1,8},{2,9},{3,10},{4,11},{5,12},{6,13},{7,14},{8,23},{9,16... | collective-permute-start | bytes 786440 | tf_op jit(solution)/shard_map/ppermute | solution.py:44
  36.6 8.4 %collective-permute-start.7 = (f32[256,256]{1,0:T(8,128)S(1)}, f32[256,256]{1,0:T(8,128)S(1)}, u32[]{:S(2)}, u32[]{:S(2)}) collective-permute-start(f32[256,256]{1,0:T(8,128)S(1)} %add.3.own), channel_id=1, source_target_pairs={{0,1},{1,0},{2,3},{3,2},{4,5},{5,4},{6,7},{7,6},{8,9},{9,8},{10,11... | collective-permute-start | bytes 786440 | tf_op jit(solution)/shard_map/ppermute | solution.py:44
  37.5 15.0 %collective-permute-start.8 = (bf16[256,512]{1,0:T(8,128)(2,1)S(1)}, bf16[256,512]{1,0:T(8,128)(2,1)S(1)}, u32[]{:S(2)}, u32[]{:S(2)}) collective-permute-start(bf16[256,512]{1,0:T(8,128)(2,1)S(1)} %shard_map.98), channel_id=1, source_target_pairs={{0,1},{1,2},{2,3},{3,4},{4,5},{5,6},{6,7},{7,0},{8,9},{9,10},{10,1... | collective-permute-start | bytes 786440 | tf_op jit(solution)/shard_map/ppermute | solution.py:44

commit v2 on v1

v2 whole, which is shorter than its diff:
```python
import jax
import jax.numpy as jnp
from jax import lax
from jax.experimental import pallas as pl
from jax.experimental.pallas import tpu as pltpu
from jax.sharding import PartitionSpec as P

F32 = jnp.float32
BF16 = jnp.bfloat16
ANY = pl.BlockSpec(memory_space=pl.ANY)
VMEM = pl.BlockSpec(memory_space=pltpu.VMEM)
SMEM = pl.BlockSpec(memory_space=pltpu.SMEM)
PANEL = 32
PIECE = 16


def dot(a, b, dims, precision=lax.Precision.HIGHEST):
    return lax.dot_general(a, b, (dims, ((), ())), precision=precision, preferred_element_type=F32)


def nn(a, b):
    return dot(a, b, ((1,), (0,)))


def tn(a, b):
    return dot(a, b, ((0,), (0,)))


def bf_nn(a, b):
    return dot(a, b, ((1,), (0,)), lax.Precision.DEFAULT)


def bf_nt(a, b):
    return dot(a, b, ((1,), (1,)), lax.Precision.DEFAULT)


def send(block, axes, sizes, partner):
    count_x, count_y = sizes
    route = []
    for i in range(count_x):
        for j in range(count_y):
            x, y = partner(i, j)
            route.append((i * count_y + j, x % count_x * count_y + y % count_y))
    return lax.ppermute(block, axes, route)


def eliminate(jobs, nb, sb):
    iota = lax.broadcasted_iota(jnp.int32, (8, 128), 0)
    groups = nb // 8
    scales = [[jnp.ones((8, 128), F32) for _ in range(groups)] for _ in jobs]
    for s in range(0, nb, sb):
        g0 = s // 8
        columns = []
        for k, tiles in jobs:
            base = (k + s) % 128
            columns.append(
                [
                    {
                        g: jnp.broadcast_to(tiles[g][0][:, base + j : base + j + 1], (8, 128))
                        for g in range(g0 + j // 8, groups)
                    }
                    for j in range(sb)
                ]
            )
        for p in range(sb):
            gp = g0 + p // 8
            r = p % 8
            for (_, tiles), cols, scale in zip(jobs, columns, scales):
                pivot = jnp.broadcast_to(cols[p][gp][r : r + 1, :], (8, 128))
                inv = 1.0 / pivot
                scale[gp] = jnp.where(iota == r, lax.rsqrt(pivot), scale[gp])
                m = {g: cols[p][g] * inv for g in range(gp, groups)}
                for j in range(p + 1, sb):
                    gj = g0 + j // 8
                    t = jnp.broadcast_to(cols[p][gj][j % 8 : j % 8 + 1, :], (8, 128))
                    for g in range(gj, groups):
                        cols[j][g] = cols[j][g] - m[g] * t
                rows = [jnp.broadcast_to(t[r : r + 1, :], (8, 128)) for t in tiles[gp]]
                for g in range(gp, groups):
                    if g == gp:
                        if r == 7:
                            continue
                        m[g] = jnp.where(iota > r, m[g], 0.0)
                    tiles[g] = [t - m[g] * w for t, w in zip(tiles[g], rows)]
    return [
        [[t * scale[g] for t in tiles[g]] for g in range(groups)] for (_, tiles), scale in zip(jobs, scales)
    ]


def factor_rows(k, reads, u_refs, w_refs, n):
    lanes = lax.broadcasted_iota(jnp.int32, (8, 128), 1)
    sub = lax.broadcasted_iota(jnp.int32, (8, 128), 0)
    nb = PANEL
    lo = k // 128 * 128
    hi = (k + nb - 1) // 128 * 128 + 128
    jobs = []
    for read, u, w in zip(reads, u_refs, w_refs):
        main = read(slice(k, k + nb), slice(lo, n))
        side = jnp.zeros((nb, hi), F32)
        cuts = [0, k - nb, k] if k > nb else [0, k]
        for c0, c1 in zip(cuts, cuts[1:]):
            if c0 < c1:
                col = u[c0:c1, k : k + nb]
                main = main - tn(col, u[c0:c1, lo:n])
                if w is not None:
                    side = side - tn(col, w[c0:c1, 0:hi])
        tiles = []
        for g in range(nb // 8):
            row = [main[8 * g : 8 * g + 8, c : c + 128] for c in range(0, n - lo, 128)]
            if w is not None:
                more = [side[8 * g : 8 * g + 8, c : c + 128] for c in range(0, hi, 128)]
                more[-1] = more[-1] + jnp.where(lanes == sub + (k + 8 * g - (hi - 128)), 1.0, 0.0)
                row += more
            tiles.append(row)
        jobs.append((k, tiles))
    na = (n - lo) // 128
    for tiles, u, w in zip(eliminate(jobs, nb, PIECE), u_refs, w_refs):
        for g in range(nb // 8):
            first = k + 8 * g
            r = slice(first, first + 8)
            for i in range(na):
                c = lo + 128 * i
                t = tiles[g][i]
                if c == lo:
                    t = jnp.where(lanes + c >= sub + first, t, 0.0)
                u[r, c : c + 128] = t
            for c in range(0, lo, 128):
                u[r, c : c + 128] = jnp.zeros((8, 128), F32)
            if w is not None:
                for i, c in enumerate(range(0, hi, 128)):
                    w[r, c : c + 128] = tiles[g][na + i]
                for c in range(hi, n, 128):
                    w[r, c : c + 128] = jnp.zeros((8, 128), F32)


def node_kernel(own, other, out, stacked):
    rank = own.shape[1]
    half = rank // 2
    parity = lax.axis_index("gx") % 2
    gram = 0.25 * (own[0:rank, :] + other[0:rank, :])
    mine = pl.multiple_of(parity * half, half)
    theirs = pl.multiple_of((1 - parity) * half, half)
    stacked[pl.ds(mine, half), :] = own[rank : rank + half, :]
    stacked[pl.ds(theirs, half), :] = other[rank : rank + half, :]
    t = stacked[...]
    right = nn(gram, t)
    out[0:half, :] = 0.25 * tn(t[:, 0:half], right)
    corner = 0.25 * tn(t[:, half:], right[:, half:])
    out[half:, 0:half] = corner[0 : half // 2]
    out[half:, half:] = corner[half // 2 :]


def leaf_kernel(gram, u, w):
    n = gram.shape[1]
    reads = [lambda r, c, m=m: gram[m, r, c] for m in range(2)]
    for k in range(0, n // 2, PANEL):
        factor_rows(k, reads, [u.at[m] for m in range(2)], [w.at[m] for m in range(2)], n)


def orthogonal_kernel(gram, basis, u_half, w_half, q, u, w):
    n = gram.shape[1]
    half = n // 2
    u[:, 0:half, :] = u_half[...]
    w[:, 0:half, :] = w_half[...]
    reads = [lambda r, c, m=m: gram[m, r, c] for m in range(2)]
    for k in range(half, n, PANEL):
        factor_rows(k, reads, [u.at[m] for m in range(2)], [w.at[m] for m in range(2)], n)
    for leaf in range(2):
        rest = w[leaf]
        total = None
        for _ in range(3):
            part = rest.astype(BF16)
            rest = rest - part.astype(F32)
            term = bf_nt(basis[0, leaf], part)
            total = term if total is None else total + term
        q[0, leaf] = total.astype(BF16)


def slot_of(slots, leaf, direction):
    found = 0
    for s in range(5):
        found = found + jnp.where(slots[0, leaf, s] == direction, s, 0)
    return found


def first_kernel(basis_h, transfer_h, node_h, slots_h, points_h, scales_h, tiles_h,
                 gram_h, sent_h, low_h, high_h, up_h, x_h, gx_a, gx_b,
                 gram, sent, acc, basis, transfer, slots, points, scales, tiles, east, west, in_sems, tile_sems, out_sems):
    rank = gram.shape[1]
    half = node_h.shape[2]
    sources = (
        (basis_h, basis), (transfer_h, transfer), (slots_h, slots), (points_h, points), (scales_h, scales),
        (node_h.at[0, 0], sent.at[pl.ds(rank, half)]),
    )
    loads = [pltpu.make_async_copy(a, b, in_sems.at[i]) for i, (a, b) in enumerate(sources)]
    for load in loads:
        load.start()

    def tile_copy(leaf, slot):
        return pltpu.make_async_copy(tiles_h.at[0, leaf, slot], tiles.at[leaf, slot], tile_sems.at[leaf, slot])

    loads[0].wait()
    loads[1].wait()
    for leaf in range(2):
        for slot in range(5):
            tile_copy(leaf, slot).start()
    total = None
    for leaf in range(2):
        b = basis[0, leaf]
        g = dot(b, b, ((0,), (0,)), lax.Precision.DEFAULT) / basis.shape[2]
        gram[leaf] = g
        t = transfer[0, leaf]
        part = tn(t, nn(g, t))
        total = part if total is None else total + part
    sent[0:rank, :] = total
    for load in loads[2:]:
        load.wait()
    waits = []

    def store(scratch, target):
        waits.append(pltpu.make_async_copy(scratch, target, out_sems.at[len(waits)]))
        waits[-1].start()

    store(gram, gram_h)
    store(sent, sent_h)
    west[0] = points[0, 0].T
    west[3] = points[0, 1].T
    east[3] = west[3]
    xt = (west.at[0], west.at[3])
    store(west.at[0], x_h)
    for leaf in range(2):
        for slot in range(5):
            tile_copy(leaf, slot).wait()

    def mirrored(leaf, d):
        slot = slot_of(slots, leaf, d)
        scaled = (xt[leaf][...].astype(F32) * scales[0, slot, pl.ds(leaf, 1), :]).astype(BF16)
        return bf_nn(scaled, tiles[leaf, slot])

    def direct(leaf, d, x):
        slot = slot_of(slots, leaf, d)
        return bf_nt(x, tiles[leaf, slot]) * scales[0, slot, pl.ds(leaf, 1), :]

    east[0] = mirrored(0, 1).astype(BF16)
    west[1] = mirrored(0, 4).astype(BF16)
    east[1] = (mirrored(0, 3) + mirrored(1, 1)).astype(BF16)
    east[2] = mirrored(1, 3).astype(BF16)
    west[2] = mirrored(1, 4).astype(BF16)
    even = lax.axis_index("gx") % 2 == 0

    @pl.when(even)
    def _():
        pltpu.make_async_copy(east, gx_a, out_sems.at[3]).start()
        pltpu.make_async_copy(west, gx_b, out_sems.at[4]).start()

    @pl.when(jnp.logical_not(even))
    def _():
        pltpu.make_async_copy(west, gx_a, out_sems.at[3]).start()
        pltpu.make_async_copy(east, gx_b, out_sems.at[4]).start()

    waits.append(pltpu.make_async_copy(east, gx_a, out_sems.at[3]))
    waits.append(pltpu.make_async_copy(west, gx_b, out_sems.at[4]))
    acc[0] = mirrored(1, 2)
    store(acc.at[0], up_h)
    acc[1] = direct(0, 0, xt[0][...]) + direct(0, 2, xt[1][...])
    store(acc.at[1], low_h)
    acc[2] = direct(1, 0, xt[1][...]) + mirrored(0, 2)
    store(acc.at[2], high_h)
    for w in waits:
        w.wait()


def sides():
    gx, gy = lax.axis_index("gx"), lax.axis_index("gy")
    last_x, last_y = lax.axis_size("gx") - 1, lax.axis_size("gy") - 1
    return gx < last_x, gx > 0, gy < last_y, gy > 0, gx % 2 == 0


def kept(inside, product):
    return jnp.where(inside, product.astype(F32), 0.0)


def up_kernel(own, a, b, out):
    east, west, _, _, even = sides()
    out[...] = (own[...] + a[2].astype(F32) + kept(jnp.where(even, west, east), b[2])).astype(BF16)


def near_top_kernel(slots, scales, tiles, low_in, high_in, gx_a, gx_b, n, n_a, n_b, own, other,
                    out, low_out, top, done, done_sem):
    east, west, north, _, even = sides()
    beside = jnp.where(even, west, east)
    pts = low_in.shape[1]
    order = top.shape[2]
    half = order // 2

    def read(r, c):
        if r.start < half:
            return own[r, c] + other[r, c]
        first = r.start - half
        shift = 0
        if first >= half // 2:
            first, shift = first - half // 2, half
        place = (slice(half + first, half + first + PANEL), slice(shift, shift + half))
        return own[place] + other[place]

    x0_east = jnp.where(even, gx_a[0], gx_b[0])
    x1_east = jnp.where(even, gx_a[3], gx_b[3])
    x1_west = jnp.where(even, gx_b[3], gx_a[3])
    ne = jnp.where(even, n_a[...], n_b[...])
    nw = jnp.where(even, n_b[...], n_a[...])
    terms = (
        ((1, x0_east, east), (3, x1_east, east), (4, x1_west, west)),
        ((1, x1_east, east), (2, n[...], north), (3, ne, north & east), (4, nw, north & west)),
    )
    pieces = [(leaf, c) for leaf in (1, 0) for c in range(0, pts, 128)]
    for i, k in enumerate(range(0, order, PANEL)):
        factor_rows(k, [read], [top.at[0, 0]], [None], order)
        leaf, c = pieces[i]
        cols = slice(c, c + 128)
        if leaf == 0:
            total = low_in[:, cols] + kept(west, jnp.where(even, gx_b[0, :, cols], gx_a[0, :, cols]))
        else:
            total = high_in[:, cols] + gx_a[1, :, cols].astype(F32) + kept(beside, gx_b[1, :, cols])
        for d, x, inside in terms[leaf]:
            slot = slot_of(slots, leaf, d)
            scale = jnp.where(inside, scales[0, slot, pl.ds(leaf, 1), cols], 0.0)
            total = total + bf_nt(x, tiles[0, leaf, slot, cols, :]) * scale
        if leaf == 0:
            low_out[:, cols] = total
        else:
            done[cols, :] = total.T.astype(BF16)
    copy = pltpu.make_async_copy(done, out.at[0, 1], done_sem)
    copy.start()
    copy.wait()


def last_kernel(near, low, south, out, done, sem):
    _, _, _, inside, _ = sides()
    done[...] = (low[...] + kept(inside, south[...])).T.astype(BF16)
    copy = pltpu.make_async_copy(done, out.at[0, 0], sem)
    copy.start()
    copy.wait()


def shape(*dims, dtype=BF16):
    return jax.ShapeDtypeStruct(dims, dtype)


def call(kernel, outs, in_specs, out_specs, scratch=(), flops=10**6, moved=1 << 10, vmem=32 << 20, aliases=None):
    return pl.pallas_call(
        kernel,
        out_shape=outs,
        in_specs=in_specs,
        out_specs=out_specs,
        scratch_shapes=list(scratch),
        input_output_aliases=aliases or {},
        compiler_params=pltpu.CompilerParams(vmem_limit_bytes=vmem),
        cost_estimate=pl.CostEstimate(flops=flops, bytes_accessed=moved, transcendentals=0),
    )


def make_shards(sizes):
    axes = ("gx", "gy")

    def shards(points_x, near_tiles, scales, slot_direction, basis, leaf_transfer, node_transfer):
        pts, vecs = points_x.shape[2:]
        rank = basis.shape[3]
        half = node_transfer.shape[2]
        dma = pltpu.SemaphoreType.DMA

        block = shape(vecs, pts)
        wide = shape(vecs, pts, dtype=F32)
        sides_sent = shape(4, vecs, pts)
        scales = jnp.transpose(scales, (0, 2, 1, 3))
        gram, sent, low, high, up, own_x, gx_a, gx_b = call(
            first_kernel,
            (
                shape(2, rank, rank, dtype=F32),
                shape(rank + half, rank, dtype=F32),
                wide, wide, wide, block, sides_sent, sides_sent,
            ),
            [ANY] * 7,
            (ANY,) * 8,
            [
                pltpu.VMEM((2, rank, rank), F32),
                pltpu.VMEM((rank + half, rank), F32),
                pltpu.VMEM((3, vecs, pts), F32),
                pltpu.VMEM(basis.shape, BF16),
                pltpu.VMEM(leaf_transfer.shape, F32),
                pltpu.SMEM(slot_direction.shape, jnp.int32),
                pltpu.VMEM(points_x.shape, BF16),
                pltpu.VMEM(scales.shape, F32),
                pltpu.VMEM(near_tiles.shape[1:], BF16),
                *[pltpu.VMEM((4, vecs, pts), BF16)] * 2,
                dma((6,)),
                dma((2, 5)),
                dma((8,)),
            ],
        )(*(pltpu.with_memory_space_constraint(a, pltpu.HBM) for a in (
            basis, leaf_transfer, node_transfer, slot_direction, points_x, scales, near_tiles)))
        got = send(sent, axes, sizes, lambda i, j: (i ^ 1, j))

        got_a = send(gx_a, axes, sizes, lambda i, j: (i ^ 1, j))
        got, got_a = lax.optimization_barrier((got, got_a))
        packed = shape(rank - rank // 4, rank, dtype=F32)
        node = call(node_kernel, packed, [VMEM] * 2, VMEM, [pltpu.VMEM((rank, rank), F32)])(sent, got)
        node_got = send(node, axes, sizes, lambda i, j: (i, j ^ 1))
        across = lambda i, j: (i - 1 if i % 2 == 0 else i + 1, j)
        got_b = send(gx_b, axes, sizes, across)
        n = send(own_x, axes, sizes, lambda i, j: (i, j - 1))
        halves = shape(2, rank // 2, rank, dtype=F32)
        u, w = call(leaf_kernel, (halves, halves), [VMEM], (VMEM, VMEM))(gram)

        w, node_got, n = lax.optimization_barrier((w, node_got, n))
        pair = node + node_got
        u, pair = lax.optimization_barrier((u, pair))
        other = send(pair, axes, sizes, lambda i, j: (i ^ 2, j))
        n_a = send(n, axes, sizes, lambda i, j: (i ^ 1, j))
        n_b = send(n, axes, sizes, across)
        square = pltpu.VMEM((2, rank, rank), F32)
        leaf_q = call(orthogonal_kernel, shape(*basis.shape), [VMEM] * 4, VMEM, [square, square])(gram, basis, u, w)

        leaf_q, got_b, other = lax.optimization_barrier((leaf_q, got_b, other))
        total_up = call(up_kernel, block, [VMEM] * 3, VMEM)(up, got_a, got_b)
        south = send(total_up, axes, sizes, lambda i, j: (i, j + 1))

        near, low, top = call(
            near_top_kernel,
            (shape(*points_x.shape), wide, shape(1, 1, rank, rank, dtype=F32)),
            [SMEM, *[VMEM] * 11],
            (ANY, VMEM, VMEM),
            [pltpu.VMEM((pts, vecs), BF16), dma],
        )(slot_direction, scales, near_tiles, low, high, got_a, got_b, n, n_a, n_b, pair, other)
        near = call(
            last_kernel,
            shape(*points_x.shape),
            [ANY, VMEM, VMEM],
            ANY,
            [pltpu.VMEM((pts, vecs), BF16), dma],
            aliases={0: 0},
        )(near, low, south)
        return near, leaf_q, top

    return shards


def solution(mesh):
    leaf = P("gx", "gy", None, None)
    placed = (leaf, P("gx", "gy", None, None, None), leaf, P("gx", "gy", None), leaf, leaf, leaf)
    return jax.shard_map(
        make_shards((mesh.shape["gx"], mesh.shape["gy"])),
        mesh=mesh,
        in_specs=placed,
        out_specs=(leaf, leaf, leaf),
        check_vma=False,
    )
```

time: 53.6 us -> 47.6 us (0.89)
  Pallas kernels: 32.6 us -> 28.4 us
  starting transfers between devices: 17.2 us -> 15.5 us
    pallas_call x5, Pallas kernels: 24.2 us -> 20.7 us  [the longest x1 8.86 us: shards(): call(near_top_kernel, (shape(*points_x.shape), wide, shape(1, 1, rank, ra...]
    ppermute x9, starting transfers between devices: 17.2 us -> 15.5 us  [send(): return lax.ppermute(block, axes, route)]
    pallas_call x1, Pallas kernels: 7.61 us -> 6.81 us  [shards(): call(first_kernel, (shape(2, rank, rank, dtype=F32), shape(rank + half, r...]
  transfers between devices with their start and end apart: 9 -> 9, of which waited for: 2 -> 2; matrix products, arithmetic and copies ran while one was open for 0% -> 0% of each run, Pallas kernels for 45% -> 44%
where the time goes in v2:
time: 47.6 us; the launch traced here: 47.2 us
  Pallas kernels  28.4 us (60%)
  starting transfers between devices  15.5 us (33%)
  waiting for transfers between devices  2.36 us (5%)
  between operations  0.9 us (2%)
    ppermute x9, starting transfers between devices, send(): return lax.ppermute(block, axes, route)  15.5 us
    pallas_call x1, Pallas kernels, shards(): call(near_top_kernel, (shape(*points_x.shape), wide, shape(1, 1, rank, ra...  8.86 us
    pallas_call x1, Pallas kernels, shards(): call(first_kernel, (shape(2, rank, rank, dtype=F32), shape(rank + half, r...  6.81 us
    pallas_call x1, Pallas kernels, shards(): call(orthogonal_kernel, shape(*basis.shape), [VMEM] * 4, VMEM, [square, s...  6.17 us
    pallas_call x1, Pallas kernels, shards(): u, w = call(leaf_kernel, (halves, halves), [VMEM], (VMEM, VMEM))(gram)  4.45 us
    ppermute x9, waiting for transfers between devices, send(): return lax.ppermute(block, axes, route)  2.36 us
    pallas_call x1, Pallas kernels, shards(): call(node_kernel, packed, [VMEM] * 2, VMEM, [pltpu.VMEM((rank, rank), F32)])  1.13 us
  transfers between devices with their start and end apart: 9, of which 2 were waited for; matrix products, arithmetic and copies ran while one was open for 0% of the time, Pallas kernels for 44%

profile of v2, /device:TPU:1, one launch (start us, length us, event | category | flops | bytes accessed | tf_op | source)
XLA Modules:
  0.0 47.2 jit_solution(4521747300876066009)
XLA Ops:
  0.6 0.0 copy-start.1
  0.6 6.8 %shard_map.94 = (f32[2,256,256]{2,1,0:T(8,128)S(1)}, f32[384,256]{1,0:T(8,128)S(1)}, f32[256,512]{1,0:T(8,128)S(1)}, f32[256,512]{1,0:T(8,128)S(1)}, f32[256,512...) custom-call(bf16[1,2,512,256]{3,2,1,0:T(8,128)(2,1)} %basis.1, ...), custom_call_target="tpu_custom_call" | custom-call | flops 1000000 | bytes 1024 | tf_op jit(solution)/shard_map/pallas_call | solution.py:375
  7.5 0.0 copy-start
  7.5 0.0 copy-start.2
  7.5 0.0 copy-start.3
  7.5 3.3 %collective-permute-start.1 = (bf16[4,256,512]{2,1,0:T(8,128)(2,1)S(1)}, bf16[4,256,512]{2,1,0:T(8,128)(2,1)S(1)}, u32[]{:S(2)}, u32[]{:S(2)}) collective-permute-start(bf16[4,256,512]{2,1,0:T(8,128)(2,1)S(1)} %get-tuple-element.29), channel_id=1, source_target_pairs={{0,8},{1,9},{2,10},{3,11},{4,12},{5,13},{6,14},{7,15},{8,0},{9,1},... | collective-permute-start | bytes 3145736 | tf_op jit(solution)/shard_map/ppermute | solution.py:44
  10.8 0.0 collective-permute-start.4
  10.8 3.6 %collective-permute-start = (f32[384,256]{1,0:T(8,128)S(1)}, f32[384,256]{1,0:T(8,128)S(1)}, u32[]{:S(2)}, u32[]{:S(2)}) collective-permute-start(f32[384,256]{1,0:T(8,128)S(1)} %get-tuple-element.28.own), channel_id=1, source_target_pairs={{0,8},{1,9},{2,10},{3,11},{4,12},{5,13},{6,14},{7,15},{8,0},{9,1},... | collective-permute-start | bytes 1179656 | tf_op jit(solution)/shard_map/ppermute | solution.py:44
  14.4 5.6 %collective-permute-start.3 = (bf16[256,512]{1,0:T(8,128)(2,1)S(1)}, bf16[256,512]{1,0:T(8,128)(2,1)S(1)}, u32[]{:S(2)}, u32[]{:S(2)}) collective-permute-start(bf16[256,512]{1,0:T(8,128)(2,1)S(1)} %get-tuple-element.35), channel_id=1, source_target_pairs={{0,7},{1,0},{2,1},{3,2},{4,3},{5,4},{6,5},{7,6},{8,15},{9,8},{10,9... | collective-permute-start | bytes 786440 | tf_op jit(solution)/shard_map/ppermute | solution.py:44
  20.0 0.0 collective-permute-done.other
  20.0 0.0 collective-permute-done.1.gx_a.a
  20.0 1.1 %shard_map.96 = f32[192,256]{1,0:T(8,128)S(1)} custom-call(f32[384,256]{1,0:T(8,128)S(1)} %get-tuple-element.28.own, f32[384,256]{1,0:T(8,128)S(1)} %collective-permute-done.other), custom_call_target="tpu_custom_call" | custom-call | flops 1000000 | bytes 1024 | tf_op jit(solution)/shard_map/pallas_call | solution.py:406
  21.1 0.1 collective-permute-start.2
  21.2 4.4 %shard_map.95 = (f32[2,128,256]{2,1,0:T(8,128)S(1)}, f32[2,128,256]{2,1,0:T(8,128)S(1)}) custom-call(f32[2,256,256]{2,1,0:T(8,128)S(1)} %get-tuple-element.31.gram), custom_call_target="tpu_custom_call" | custom-call | flops 1000000 | bytes 1024 | tf_op jit(solution)/shard_map/pallas_call | solution.py:412
  25.7 0.0 collective-permute-done.3.n
  25.7 1.7 %collective-permute-done.2 = f32[192,256]{1,0:T(8,128)S(1)} collective-permute-done((f32[192,256]{1,0:T(8,128)S(1)}, f32[192,256]{1,0:T(8,128)S(1)}, u32[]{:S(2)}, u32[]{:S(2)}) %collective-permute-start.2) | collective-permute-done | bytes 196640 | tf_op jit(solution)/shard_map/ppermute | solution.py:44
  27.5 0.1 collective-permute-start.5
  27.6 1.4 %collective-permute-start.6 = (bf16[256,512]{1,0:T(8,128)(2,1)S(1)}, bf16[256,512]{1,0:T(8,128)(2,1)S(1)}, u32[]{:S(2)}, u32[]{:S(2)}) collective-permute-start(bf16[256,512]{1,0:T(8,128)(2,1)S(1)} %collective-permute-done.3.n), channel_id=1, source_target_pairs={{0,8},{1,9},{2,10},{3,11},{4,12},{5,13},{6,14},{7,15},{8,0},{9,1},... | collective-permute-start | bytes 786440 | tf_op jit(solution)/shard_map/ppermute | solution.py:44
  28.9 1.4 %collective-permute-start.7 = (bf16[256,512]{1,0:T(8,128)(2,1)S(1)}, bf16[256,512]{1,0:T(8,128)(2,1)S(1)}, u32[]{:S(2)}, u32[]{:S(2)}) collective-permute-start(bf16[256,512]{1,0:T(8,128)(2,1)S(1)} %collective-permute-done.3.n), channel_id=1, source_target_pairs={{0,248},{1,249},{2,250},{3,251},{4,252},{5,253},{6,254},{7,255},{8... | collective-permute-start | bytes 786440 | tf_op jit(solution)/shard_map/ppermute | solution.py:44
  30.3 0.0 copy-done.1
  30.3 6.2 %shard_map.97 = bf16[1,2,512,256]{3,2,1,0:T(8,128)(2,1)} custom-call(f32[2,256,256]{2,1,0:T(8,128)S(1)} %get-tuple-element.31.gram, bf16[1,2,512,256]{3,2,1,0:T(8,128)(2,1)S(1)} %copy-done.1, f32[2,128,256]{2,1,0:T(8,128)S(1)} %get-tuple-element.37.u_half, f32[2,128,256]{2,1,0:T(8,128)S(1)} %get-tuple-element.38.w_half), custom_call_target="tpu_custom_call" | custom-call | flops 1000000 | bytes 1024 | tf_op jit(solution)/shard_map/pallas_call | solution.py:421
  36.5 0.0 collective-permute-done.4.gx_b.b
  36.5 0.0 collective-permute-done.5.other
  36.5 0.1 shard_map.99
  36.6 0.1 collective-permute-start.8
  36.7 0.0 collective-permute-done.6.n_a
  36.7 0.6 %collective-permute-done.7.n_b = bf16[256,512]{1,0:T(8,128)(2,1)S(1)} collective-permute-done((bf16[256,512]{1,0:T(8,128)(2,1)S(1)}, bf16[256,512]{1,0:T(8,128)(2,1)S(1)}, u32[]{:S(2)}, u32[]{:S(2)}) %collective-permute-start.7) | collective-permute-done | bytes 262176 | tf_op jit(solution)/shard_map/ppermute | solution.py:44
  37.3 0.0 copy-done
  37.3 0.0 copy-done.2
  37.3 0.0 copy-done.3
  37.3 8.9 %shard_map.98 = (bf16[1,2,512,256]{3,2,1,0:T(8,128)(2,1)}, f32[256,512]{1,0:T(8,128)S(1)}, f32[1,1,256,256]{3,2,1,0:T(8,128)}) custom-call(s32[1,2,5]{2,1,0:T(2,128)S(1)} %copy-done.3, f32[1,5,2,512]{3,2,1,0:T(2,128)S(1)} %bitcast.2, bf16[1,2,5,512,512]{4,3,2,1,0:T(8,128)(2,1)S(1)} %copy-done, f32[256,512]{1,0:T(8,128)S(1)} %get-tuple-element.26.low_in, ...), custom_call_target="tpu_custom_call" | custom-call | flops 1000000 | bytes 1024 | tf_op jit(solution)/shard_map/pallas_call | solution.py:427
  46.2 0.0 collective-permute-done.8.south
  46.2 0.9 %shard_map.100 = bf16[1,2,512,256]{3,2,1,0:T(8,128)(2,1)} custom-call(bf16[1,2,512,256]{3,2,1,0:T(8,128)(2,1)} %get-tuple-element.44.near, f32[256,512]{1,0:T(8,128)S(1)} %get-tuple-element.45.low, bf16[256,512]{1,0:T(8,128)(2,1)S(1)} %collective-permute-done.8.south), custom_call_target="tpu_custom_call", output_to_operand_aliasing={{}: (0, {})} | custom-call | flops 1000000 | bytes 1024 | tf_op jit(solution)/shard_map/pallas_call | solution.py:434
  (1 shorter events, 0.0 us)
Async XLA Ops:
  0.6 29.7 %copy-start.1 = (bf16[1,2,512,256]{3,2,1,0:T(8,128)(2,1)S(1)}, bf16[1,2,512,256]{3,2,1,0:T(8,128)(2,1)}, u32[]{:S(2)}) copy-start(bf16[1,2,512,256]{3,2,1,0:T(8,128)(2,1)} %basis.1) | copy-start | bytes 1572868
  7.5 29.8 %copy-start = (bf16[1,2,5,512,512]{4,3,2,1,0:T(8,128)(2,1)S(1)}, bf16[1,2,5,512,512]{4,3,2,1,0:T(8,128)(2,1)}, u32[]{:S(2)}) copy-start(bf16[1,2,5,512,512]{4,3,2,1,0:T(8,128)(2,1)} %tiles.1) | copy-start | bytes 15728644
  7.5 29.8 %copy-start.2 = (f32[1,2,5,512]{3,1,2,0:T(2,128)S(1)}, f32[1,2,5,512]{3,1,2,0:T(2,128)}, u32[]{:S(2)}) copy-start(f32[1,2,5,512]{3,1,2,0:T(2,128)} %param.9) | copy-start | bytes 61444
  7.5 29.8 %copy-start.3 = (s32[1,2,5]{2,1,0:T(2,128)S(1)}, s32[1,2,5]{2,1,0:T(2,128)}, u32[]{:S(2)}) copy-start(s32[1,2,5]{2,1,0:T(2,128)} %slots.1) | copy-start | bytes 124
  7.5 12.5 %collective-permute-start.1 = (bf16[4,256,512]{2,1,0:T(8,128)(2,1)S(1)}, bf16[4,256,512]{2,1,0:T(8,128)(2,1)S(1)}, u32[]{:S(2)}, u32[]{:S(2)}) collective-permute-start(bf16[4,256,512]{2,1,0:T(8,128)(2,1)S(1)} %get-tuple-element.29), channel_id=1, source_target_pairs={{0,8},{1,9},{2,10},{3,11},{4,12},{5,13},{6,14},{7,15},{8,0},{9,1},... | collective-permute-start | bytes 3145736 | tf_op jit(solution)/shard_map/ppermute | solution.py:44
  10.8 25.6 %collective-permute-start.4 = (bf16[4,256,512]{2,1,0:T(8,128)(2,1)S(1)}, bf16[4,256,512]{2,1,0:T(8,128)(2,1)S(1)}, u32[]{:S(2)}, u32[]{:S(2)}) collective-permute-start(bf16[4,256,512]{2,1,0:T(8,128)(2,1)S(1)} %get-tuple-element.39), channel_id=1, source_target_pairs={{0,248},{1,249},{2,250},{3,251},{4,252},{5,253},{6,254},{7,255},{8... | collective-permute-start | bytes 3145736 | tf_op jit(solution)/shard_map/ppermute | solution.py:44
  10.8 9.2 %collective-permute-start = (f32[384,256]{1,0:T(8,128)S(1)}, f32[384,256]{1,0:T(8,128)S(1)}, u32[]{:S(2)}, u32[]{:S(2)}) collective-permute-start(f32[384,256]{1,0:T(8,128)S(1)} %get-tuple-element.28.own), channel_id=1, source_target_pairs={{0,8},{1,9},{2,10},{3,11},{4,12},{5,13},{6,14},{7,15},{8,0},{9,1},... | collective-permute-start | bytes 1179656 | tf_op jit(solution)/shard_map/ppermute | solution.py:44
  14.4 11.3 %collective-permute-start.3 = (bf16[256,512]{1,0:T(8,128)(2,1)S(1)}, bf16[256,512]{1,0:T(8,128)(2,1)S(1)}, u32[]{:S(2)}, u32[]{:S(2)}) collective-permute-start(bf16[256,512]{1,0:T(8,128)(2,1)S(1)} %get-tuple-element.35), channel_id=1, source_target_pairs={{0,7},{1,0},{2,1},{3,2},{4,3},{5,4},{6,5},{7,6},{8,15},{9,8},{10,9... | collective-permute-start | bytes 786440 | tf_op jit(solution)/shard_map/ppermute | solution.py:44
  21.1 6.3 %collective-permute-start.2 = (f32[192,256]{1,0:T(8,128)S(1)}, f32[192,256]{1,0:T(8,128)S(1)}, u32[]{:S(2)}, u32[]{:S(2)}) collective-permute-start(f32[192,256]{1,0:T(8,128)S(1)} %shard_map.96), channel_id=1, source_target_pairs={{0,1},{1,0},{2,3},{3,2},{4,5},{5,4},{6,7},{7,6},{8,9},{9,8},{10,11... | collective-permute-start | bytes 589832 | tf_op jit(solution)/shard_map/ppermute | solution.py:44
  27.5 9.0 %collective-permute-start.5 = (f32[192,256]{1,0:T(8,128)S(1)}, f32[192,256]{1,0:T(8,128)S(1)}, u32[]{:S(2)}, u32[]{:S(2)}) collective-permute-start(f32[192,256]{1,0:T(8,128)S(1)} %add.3.own), channel_id=1, source_target_pairs={{0,16},{1,17},{2,18},{3,19},{4,20},{5,21},{6,22},{7,23},{8,24},{9,... | collective-permute-start | bytes 589832 | tf_op jit(solution)/shard_map/ppermute | solution.py:44
  27.6 9.1 %collective-permute-start.6 = (bf16[256,512]{1,0:T(8,128)(2,1)S(1)}, bf16[256,512]{1,0:T(8,128)(2,1)S(1)}, u32[]{:S(2)}, u32[]{:S(2)}) collective-permute-start(bf16[256,512]{1,0:T(8,128)(2,1)S(1)} %collective-permute-done.3.n), channel_id=1, source_target_pairs={{0,8},{1,9},{2,10},{3,11},{4,12},{5,13},{6,14},{7,15},{8,0},{9,1},... | collective-permute-start | bytes 786440 | tf_op jit(solution)/shard_map/ppermute | solution.py:44
  28.9 8.3 %collective-permute-start.7 = (bf16[256,512]{1,0:T(8,128)(2,1)S(1)}, bf16[256,512]{1,0:T(8,128)(2,1)S(1)}, u32[]{:S(2)}, u32[]{:S(2)}) collective-permute-start(bf16[256,512]{1,0:T(8,128)(2,1)S(1)} %collective-permute-done.3.n), channel_id=1, source_target_pairs={{0,248},{1,249},{2,250},{3,251},{4,252},{5,253},{6,254},{7,255},{8... | collective-permute-start | bytes 786440 | tf_op jit(solution)/shard_map/ppermute | solution.py:44
  36.6 9.6 %collective-permute-start.8 = (bf16[256,512]{1,0:T(8,128)(2,1)S(1)}, bf16[256,512]{1,0:T(8,128)(2,1)S(1)}, u32[]{:S(2)}, u32[]{:S(2)}) collective-permute-start(bf16[256,512]{1,0:T(8,128)(2,1)S(1)} %shard_map.99), channel_id=1, source_target_pairs={{0,1},{1,2},{2,3},{3,4},{4,5},{5,6},{6,7},{7,0},{8,9},{9,10},{10,1... | collective-permute-start | bytes 786440 | tf_op jit(solution)/shard_map/ppermute | solution.py:44

commit v3 on v2

--- a/solution.py
+++ b/solution.py
@@ -12,6 +12,7 @@
 SMEM = pl.BlockSpec(memory_space=pltpu.SMEM)
 PANEL = 32
 PIECE = 16
+FIRST_ROWS = 160
 
 
 def dot(a, b, dims, precision=lax.Precision.HIGHEST):
@@ -153,17 +154,16 @@
 def leaf_kernel(gram, u, w):
     n = gram.shape[1]
     reads = [lambda r, c, m=m: gram[m, r, c] for m in range(2)]
-    for k in range(0, n // 2, PANEL):
+    for k in range(0, FIRST_ROWS, PANEL):
         factor_rows(k, reads, [u.at[m] for m in range(2)], [w.at[m] for m in range(2)], n)
 
 
-def orthogonal_kernel(gram, basis, u_half, w_half, q, u, w):
+def orthogonal_kernel(gram, basis, u_first, w_first, q, u, w):
     n = gram.shape[1]
-    half = n // 2
-    u[:, 0:half, :] = u_half[...]
-    w[:, 0:half, :] = w_half[...]
+    u[:, 0:FIRST_ROWS, :] = u_first[...]
+    w[:, 0:FIRST_ROWS, :] = w_first[...]
     reads = [lambda r, c, m=m: gram[m, r, c] for m in range(2)]
-    for k in range(half, n, PANEL):
+    for k in range(FIRST_ROWS, n, PANEL):
         factor_rows(k, reads, [u.at[m] for m in range(2)], [w.at[m] for m in range(2)], n)
     for leaf in range(2):
         rest = w[leaf]
@@ -184,8 +184,8 @@
 
 
 def first_kernel(basis_h, transfer_h, node_h, slots_h, points_h, scales_h, tiles_h,
-                 gram_h, sent_h, low_h, high_h, up_h, x_h, gx_a, gx_b,
-                 gram, sent, acc, basis, transfer, slots, points, scales, tiles, east, west, in_sems, tile_sems, out_sems):
+                 gram_h, sent_h, x_h, gx_a, gx_b,
+                 gram, sent, basis, transfer, slots, points, scales, tiles, east, west, in_sems, tile_sems, out_sems):
     rank = gram.shape[1]
     half = node_h.shape[2]
     sources = (
@@ -204,15 +204,11 @@
     for leaf in range(2):
         for slot in range(5):
             tile_copy(leaf, slot).start()
-    total = None
     for leaf in range(2):
         b = basis[0, leaf]
-        g = dot(b, b, ((0,), (0,)), lax.Precision.DEFAULT) / basis.shape[2]
-        gram[leaf] = g
-        t = transfer[0, leaf]
-        part = tn(t, nn(g, t))
-        total = part if total is None else total + part
-    sent[0:rank, :] = total
+        gram[leaf] = dot(b, b, ((0,), (0,)), lax.Precision.DEFAULT) / basis.shape[2]
+    right = [nn(gram[leaf], transfer[0, leaf]) for leaf in range(2)]
+    sent[0:rank, :] = tn(transfer[0, 0], right[0]) + tn(transfer[0, 1], right[1])
     for load in loads[2:]:
         load.wait()
     waits = []
@@ -237,10 +233,6 @@
         scaled = (xt[leaf][...].astype(F32) * scales[0, slot, pl.ds(leaf, 1), :]).astype(BF16)
         return bf_nn(scaled, tiles[leaf, slot])
 
-    def direct(leaf, d, x):
-        slot = slot_of(slots, leaf, d)
-        return bf_nt(x, tiles[leaf, slot]) * scales[0, slot, pl.ds(leaf, 1), :]
-
     east[0] = mirrored(0, 1).astype(BF16)
     west[1] = mirrored(0, 4).astype(BF16)
     east[1] = (mirrored(0, 3) + mirrored(1, 1)).astype(BF16)
@@ -260,14 +252,25 @@
 
     waits.append(pltpu.make_async_copy(east, gx_a, out_sems.at[3]))
     waits.append(pltpu.make_async_copy(west, gx_b, out_sems.at[4]))
-    acc[0] = mirrored(1, 2)
-    store(acc.at[0], up_h)
-    acc[1] = direct(0, 0, xt[0][...]) + direct(0, 2, xt[1][...])
-    store(acc.at[1], low_h)
-    acc[2] = direct(1, 0, xt[1][...]) + mirrored(0, 2)
-    store(acc.at[2], high_h)
     for w in waits:
         w.wait()
+
+
+def own_kernel(slots, scales, tiles, x0, gx_a, low, high, up):
+    xt = (x0[...], gx_a[3])
+
+    def mirrored(leaf, d):
+        slot = slot_of(slots, leaf, d)
+        scaled = (xt[leaf].astype(F32) * scales[0, slot, pl.ds(leaf, 1), :]).astype(BF16)
+        return bf_nn(scaled, tiles[0, leaf, slot])
+
+    def direct(leaf, d, x):
+        slot = slot_of(slots, leaf, d)
+        return bf_nt(x, tiles[0, leaf, slot]) * scales[0, slot, pl.ds(leaf, 1), :]
+
+    low[...] = direct(0, 0, xt[0]) + direct(0, 2, xt[1])
+    high[...] = direct(1, 0, xt[1]) + mirrored(0, 2)
+    up[...] = mirrored(1, 2)
 
 
 def sides():
@@ -372,19 +375,18 @@
         wide = shape(vecs, pts, dtype=F32)
         sides_sent = shape(4, vecs, pts)
         scales = jnp.transpose(scales, (0, 2, 1, 3))
-        gram, sent, low, high, up, own_x, gx_a, gx_b = call(
+        gram, sent, own_x, gx_a, gx_b = call(
             first_kernel,
             (
                 shape(2, rank, rank, dtype=F32),
                 shape(rank + half, rank, dtype=F32),
-                wide, wide, wide, block, sides_sent, sides_sent,
+                block, sides_sent, sides_sent,
             ),
             [ANY] * 7,
-            (ANY,) * 8,
+            (ANY,) * 5,
             [
                 pltpu.VMEM((2, rank, rank), F32),
                 pltpu.VMEM((rank + half, rank), F32),
-                pltpu.VMEM((3, vecs, pts), F32),
                 pltpu.VMEM(basis.shape, BF16),
                 pltpu.VMEM(leaf_transfer.shape, F32),
                 pltpu.SMEM(slot_direction.shape, jnp.int32),
@@ -394,22 +396,28 @@
                 *[pltpu.VMEM((4, vecs, pts), BF16)] * 2,
                 dma((6,)),
                 dma((2, 5)),
-                dma((8,)),
+                dma((5,)),
             ],
         )(*(pltpu.with_memory_space_constraint(a, pltpu.HBM) for a in (
             basis, leaf_transfer, node_transfer, slot_direction, points_x, scales, near_tiles)))
         got = send(sent, axes, sizes, lambda i, j: (i ^ 1, j))
 
         got_a = send(gx_a, axes, sizes, lambda i, j: (i ^ 1, j))
-        got, got_a = lax.optimization_barrier((got, got_a))
+        low, high, up = call(own_kernel, (wide, wide, wide), [SMEM, *[VMEM] * 4], (VMEM, VMEM, VMEM), flops=2 * 10**9)(
+            slot_direction, scales, near_tiles, own_x, gx_a)
+        got, got_a, low = lax.optimization_barrier((got, got_a, low))
         packed = shape(rank - rank // 4, rank, dtype=F32)
         node = call(node_kernel, packed, [VMEM] * 2, VMEM, [pltpu.VMEM((rank, rank), F32)])(sent, got)
         node_got = send(node, axes, sizes, lambda i, j: (i, j ^ 1))
-        across = lambda i, j: (i - 1 if i % 2 == 0 else i + 1, j)
+
+        def across(i, j):
+            other = i - 1 if i % 2 == 0 else i + 1
+            return (other, j) if 0 <= other < sizes[0] else (i, j + 1)
+
         got_b = send(gx_b, axes, sizes, across)
         n = send(own_x, axes, sizes, lambda i, j: (i, j - 1))
-        halves = shape(2, rank // 2, rank, dtype=F32)
-        u, w = call(leaf_kernel, (halves, halves), [VMEM], (VMEM, VMEM))(gram)
+        firsts = shape(2, FIRST_ROWS, rank, dtype=F32)
+        u, w = call(leaf_kernel, (firsts, firsts), [VMEM], (VMEM, VMEM))(gram)
 
         w, node_got, n = lax.optimization_barrier((w, node_got, n))
         pair = node + node_got

time: 47.6 us -> 46.8 us (0.983)
  waiting for transfers between devices: 2.36 us -> 1.06 us
  starting transfers between devices: 15.5 us -> 16.1 us
    pallas_call x1 -> x2, Pallas kernels: 4.45 us -> 6.76 us  [the longest x1 5.33 us: shards(): u, w = call(leaf_kernel, (firsts, firsts), [VMEM], (VMEM, VMEM))(gram)]
    ppermute x9, waiting for transfers between devices: 2.36 us -> 1.06 us  [send(): return lax.ppermute(block, axes, route)]
    pallas_call x1, Pallas kernels: 6.17 us -> 5.1 us  [shards(): call(orthogonal_kernel, shape(*basis.shape), [VMEM] * 4, VMEM, [square, s...]
    pallas_call x1, Pallas kernels: 6.81 us -> 5.8 us  [shards(): call(first_kernel, (shape(2, rank, rank, dtype=F32), shape(rank + half, r...]
    ppermute x9, starting transfers between devices: 15.5 us -> 16.1 us  [send(): return lax.ppermute(block, axes, route)]
  transfers between devices with their start and end apart: 9 -> 9, of which waited for: 2 -> 2; matrix products, arithmetic and copies ran while one was open for 0% -> 0% of each run, Pallas kernels for 44% -> 47%
where the time goes in v3:
time: 46.8 us; the launch traced here: 46.7 us
  Pallas kernels  28.6 us (61%)
  starting transfers between devices  16.1 us (34%)
  waiting for transfers between devices  1.06 us (2%)
  between operations  0.93 us (2%)
    ppermute x9, starting transfers between devices, send(): return lax.ppermute(block, axes, route)  16.1 us
    pallas_call x1, Pallas kernels, shards(): call(near_top_kernel, (shape(*points_x.shape), wide, shape(1, 1, rank, ra...  8.84 us
    pallas_call x1, Pallas kernels, shards(): call(first_kernel, (shape(2, rank, rank, dtype=F32), shape(rank + half, r...  5.8 us
    pallas_call x1, Pallas kernels, shards(): u, w = call(leaf_kernel, (firsts, firsts), [VMEM], (VMEM, VMEM))(gram)  5.33 us
    pallas_call x1, Pallas kernels, shards(): call(orthogonal_kernel, shape(*basis.shape), [VMEM] * 4, VMEM, [square, s...  5.1 us
    pallas_call x1, Pallas kernels, shards(): call(own_kernel, (wide, wide, wide), [SMEM, *[VMEM] * 4], (VMEM, VMEM, VM...  1.43 us
    pallas_call x1, Pallas kernels, shards(): call(node_kernel, packed, [VMEM] * 2, VMEM, [pltpu.VMEM((rank, rank), F32)])  1.14 us
    ppermute x9, waiting for transfers between devices, send(): return lax.ppermute(block, axes, route)  1.06 us
  transfers between devices with their start and end apart: 9, of which 2 were waited for; matrix products, arithmetic and copies ran while one was open for 0% of the time, Pallas kernels for 47%

profile of v3, /device:TPU:1, one launch (start us, length us, event | category | flops | bytes accessed | tf_op | source)
XLA Modules:
  0.0 46.7 jit_solution(2769148823381280422)
XLA Ops:
  0.6 0.0 copy-start.2
  0.6 0.0 copy-start.3
  0.7 0.0 copy-start
  0.7 5.8 %shard_map.94 = (f32[2,256,256]{2,1,0:T(8,128)S(1)}, f32[384,256]{1,0:T(8,128)S(1)}, bf16[256,512]{1,0:T(8,128)(2,1)S(1)}, bf16[4,256,512]{2,1,0:T(8,128)(2,1)S(1)}, bf16[4,256,512]{2,1,0:T(8,128)(2,1)S(1)}) custom-call(bf16[1,2,512,256]{3,2,1,0:T(8,128)(2,1)} %basis.1, f32[1,2,256,256]{3,2,1,0:T(8,128)} %transfer_h.1, f32[1,1,128,256]{3,2,1,0:T(8,128)} %node_h.1, ...), custom_call_target="tpu_custom_call" | custom-call | flops 1000000 | bytes 1024 | tf_op jit(solution)/shard_map/pallas_call | solution.py:378
  6.5 0.0 copy-start.1
  6.5 3.3 %collective-permute-start.1 = (bf16[4,256,512]{2,1,0:T(8,128)(2,1)S(1)}, bf16[4,256,512]{2,1,0:T(8,128)(2,1)S(1)}, u32[]{:S(2)}, u32[]{:S(2)}) collective-permute-start(bf16[4,256,512]{2,1,0:T(8,128)(2,1)S(1)} %get-tuple-element.28.gx_a), channel_id=1, source_target_pairs={{0,8},{1,9},{2,10},{3,11},{4,12},{5,13},{6,14},{7,15},{8,0},{9,1},... | collective-permute-start | bytes 3145736 | tf_op jit(solution)/shard_map/ppermute | solution.py:45
  9.8 0.0 collective-permute-start.4
  9.8 0.3 collective-permute-start
  10.1 4.8 %collective-permute-start.3 = (bf16[256,512]{1,0:T(8,128)(2,1)S(1)}, bf16[256,512]{1,0:T(8,128)(2,1)S(1)}, u32[]{:S(2)}, u32[]{:S(2)}) collective-permute-start(bf16[256,512]{1,0:T(8,128)(2,1)S(1)} %get-tuple-element.29.x0), channel_id=1, source_target_pairs={{0,7},{1,0},{2,1},{3,2},{4,3},{5,4},{6,5},{7,6},{8,15},{9,8},{10,9... | collective-permute-start | bytes 786440 | tf_op jit(solution)/shard_map/ppermute | solution.py:45
  14.9 0.0 copy-done.2
  14.9 0.0 copy-done.3
  14.9 0.0 copy-done
  14.9 1.4 %shard_map.95 = (f32[256,512]{1,0:T(8,128)S(1)}, f32[256,512]{1,0:T(8,128)S(1)}, f32[256,512]{1,0:T(8,128)S(1)}) custom-call(s32[1,2,5]{2,1,0:T(2,128)S(1)} %copy-done.3, f32[1,5,2,512]{3,2,1,0:T(2,128)S(1)} %bitcast.2, bf16[1,2,5,512,512]{4,3,2,1,0:T(8,128)(2,1)S(1)} %copy-done, bf16[256,512]{1,0:T(8,128)(2,1)S(1)} %get-tuple-element.29.x0, ...), custom_call_target="tpu_custom_call" | custom-call | flops 2000000000 | bytes 1024 | tf_op jit(solution)/shard_map/pallas_call | solution.py:406
  16.4 0.0 collective-permute-done.other
  16.4 0.0 collective-permute-done.1.gx_a.a
  16.4 1.1 %shard_map.97 = f32[192,256]{1,0:T(8,128)S(1)} custom-call(f32[384,256]{1,0:T(8,128)S(1)} %get-tuple-element.27.own, f32[384,256]{1,0:T(8,128)S(1)} %collective-permute-done.other), custom_call_target="tpu_custom_call" | custom-call | flops 1000000 | bytes 1024 | tf_op jit(solution)/shard_map/pallas_call | solution.py:410
  17.5 0.3 collective-permute-start.2
  17.8 5.3 %shard_map.96 = (f32[2,160,256]{2,1,0:T(8,128)S(1)}, f32[2,160,256]{2,1,0:T(8,128)S(1)}) custom-call(f32[2,256,256]{2,1,0:T(8,128)S(1)} %get-tuple-element.34.gram), custom_call_target="tpu_custom_call" | custom-call | flops 1000000 | bytes 1024 | tf_op jit(solution)/shard_map/pallas_call | solution.py:420
  23.1 0.0 collective-permute-done.3.n
  23.2 0.3 collective-permute-done.2
  23.5 1.4 %collective-permute-start.5 = (f32[192,256]{1,0:T(8,128)S(1)}, f32[192,256]{1,0:T(8,128)S(1)}, u32[]{:S(2)}, u32[]{:S(2)}) collective-permute-start(f32[192,256]{1,0:T(8,128)S(1)} %add.3.own), channel_id=1, source_target_pairs={{0,16},{1,17},{2,18},{3,19},{4,20},{5,21},{6,22},{7,23},{8,24},{9,... | collective-permute-start | bytes 589832 | tf_op jit(solution)/shard_map/ppermute | solution.py:45
  24.8 2.0 %collective-permute-start.6 = (bf16[256,512]{1,0:T(8,128)(2,1)S(1)}, bf16[256,512]{1,0:T(8,128)(2,1)S(1)}, u32[]{:S(2)}, u32[]{:S(2)}) collective-permute-start(bf16[256,512]{1,0:T(8,128)(2,1)S(1)} %collective-permute-done.3.n), channel_id=1, source_target_pairs={{0,8},{1,9},{2,10},{3,11},{4,12},{5,13},{6,14},{7,15},{8,0},{9,1},... | collective-permute-start | bytes 786440 | tf_op jit(solution)/shard_map/ppermute | solution.py:45
  26.8 1.5 %collective-permute-start.7 = (bf16[256,512]{1,0:T(8,128)(2,1)S(1)}, bf16[256,512]{1,0:T(8,128)(2,1)S(1)}, u32[]{:S(2)}, u32[]{:S(2)}) collective-permute-start(bf16[256,512]{1,0:T(8,128)(2,1)S(1)} %collective-permute-done.3.n), channel_id=1, source_target_pairs={{0,1},{1,2},{2,3},{3,4},{4,5},{5,6},{6,7},{7,0},{8,16},{9,17},{10,... | collective-permute-start | bytes 786440 | tf_op jit(solution)/shard_map/ppermute | solution.py:45
  28.4 0.0 copy-done.1
  28.4 5.1 %shard_map.98 = bf16[1,2,512,256]{3,2,1,0:T(8,128)(2,1)} custom-call(f32[2,256,256]{2,1,0:T(8,128)S(1)} %get-tuple-element.34.gram, bf16[1,2,512,256]{3,2,1,0:T(8,128)(2,1)S(1)} %copy-done.1, f32[2,160,256]{2,1,0:T(8,128)S(1)} %get-tuple-element.39.u_first, f32[2,160,256]{2,1,0:T(8,128)S(1)} %get-tuple-element.40.w_first), custom_call_target="tpu_custom_call" | custom-call | flops 1000000 | bytes 1024 | tf_op jit(solution)/shard_map/pallas_call | solution.py:429
  33.5 0.0 collective-permute-done.4.gx_b.b
  33.5 0.0 collective-permute-done.5.other
  33.5 0.1 shard_map.100
  33.6 2.5 %collective-permute-start.8 = (bf16[256,512]{1,0:T(8,128)(2,1)S(1)}, bf16[256,512]{1,0:T(8,128)(2,1)S(1)}, u32[]{:S(2)}, u32[]{:S(2)}) collective-permute-start(bf16[256,512]{1,0:T(8,128)(2,1)S(1)} %shard_map.100), channel_id=1, source_target_pairs={{0,1},{1,2},{2,3},{3,4},{4,5},{5,6},{6,7},{7,0},{8,9},{9,10},{10,1... | collective-permute-start | bytes 786440 | tf_op jit(solution)/shard_map/ppermute | solution.py:45
  36.1 0.0 collective-permute-done.6.n_a
  36.1 0.0 collective-permute-done.7.n_b
  36.1 8.8 %shard_map.99 = (bf16[1,2,512,256]{3,2,1,0:T(8,128)(2,1)}, f32[256,512]{1,0:T(8,128)S(1)}, f32[1,1,256,256]{3,2,1,0:T(8,128)}) custom-call(s32[1,2,5]{2,1,0:T(2,128)S(1)} %copy-done.3, f32[1,5,2,512]{3,2,1,0:T(2,128)S(1)} %bitcast.3, bf16[1,2,5,512,512]{4,3,2,1,0:T(8,128)(2,1)S(1)} %copy-done, f32[256,512]{1,0:T(8,128)S(1)} %get-tuple-element.31.low_in, ...), custom_call_target="tpu_custom_call" | custom-call | flops 1000000 | bytes 1024 | tf_op jit(solution)/shard_map/pallas_call | solution.py:435
  44.9 0.8 %collective-permute-done.8.south = bf16[256,512]{1,0:T(8,128)(2,1)S(1)} collective-permute-done((bf16[256,512]{1,0:T(8,128)(2,1)S(1)}, bf16[256,512]{1,0:T(8,128)(2,1)S(1)}, u32[]{:S(2)}, u32[]{:S(2)}) %collective-permute-start.8) | collective-permute-done | bytes 262176 | tf_op jit(solution)/shard_map/ppermute | solution.py:45
  45.7 0.9 %shard_map.101 = bf16[1,2,512,256]{3,2,1,0:T(8,128)(2,1)} custom-call(bf16[1,2,512,256]{3,2,1,0:T(8,128)(2,1)} %get-tuple-element.46.near, f32[256,512]{1,0:T(8,128)S(1)} %get-tuple-element.47.low, bf16[256,512]{1,0:T(8,128)(2,1)S(1)} %collective-permute-done.8.south), custom_call_target="tpu_custom_call", output_to_operand_aliasing={{}: (0, {})} | custom-call | flops 1000000 | bytes 1024 | tf_op jit(solution)/shard_map/pallas_call | solution.py:442
  (1 shorter events, 0.0 us)
Async XLA Ops:
  0.6 14.3 %copy-start.2 = (f32[1,2,5,512]{3,1,2,0:T(2,128)S(1)}, f32[1,2,5,512]{3,1,2,0:T(2,128)}, u32[]{:S(2)}) copy-start(f32[1,2,5,512]{3,1,2,0:T(2,128)} %param.9) | copy-start | bytes 61444
  0.6 14.3 %copy-start.3 = (s32[1,2,5]{2,1,0:T(2,128)S(1)}, s32[1,2,5]{2,1,0:T(2,128)}, u32[]{:S(2)}) copy-start(s32[1,2,5]{2,1,0:T(2,128)} %slots.3) | copy-start | bytes 124
  0.7 14.3 %copy-start = (bf16[1,2,5,512,512]{4,3,2,1,0:T(8,128)(2,1)S(1)}, bf16[1,2,5,512,512]{4,3,2,1,0:T(8,128)(2,1)}, u32[]{:S(2)}) copy-start(bf16[1,2,5,512,512]{4,3,2,1,0:T(8,128)(2,1)} %tiles.3) | copy-start | bytes 15728644
  6.5 21.9 %copy-start.1 = (bf16[1,2,512,256]{3,2,1,0:T(8,128)(2,1)S(1)}, bf16[1,2,512,256]{3,2,1,0:T(8,128)(2,1)}, u32[]{:S(2)}) copy-start(bf16[1,2,512,256]{3,2,1,0:T(8,128)(2,1)} %basis.1) | copy-start | bytes 1572868
  6.5 9.9 %collective-permute-start.1 = (bf16[4,256,512]{2,1,0:T(8,128)(2,1)S(1)}, bf16[4,256,512]{2,1,0:T(8,128)(2,1)S(1)}, u32[]{:S(2)}, u32[]{:S(2)}) collective-permute-start(bf16[4,256,512]{2,1,0:T(8,128)(2,1)S(1)} %get-tuple-element.28.gx_a), channel_id=1, source_target_pairs={{0,8},{1,9},{2,10},{3,11},{4,12},{5,13},{6,14},{7,15},{8,0},{9,1},... | collective-permute-start | bytes 3145736 | tf_op jit(solution)/shard_map/ppermute | solution.py:45
  9.8 23.7 %collective-permute-start.4 = (bf16[4,256,512]{2,1,0:T(8,128)(2,1)S(1)}, bf16[4,256,512]{2,1,0:T(8,128)(2,1)S(1)}, u32[]{:S(2)}, u32[]{:S(2)}) collective-permute-start(bf16[4,256,512]{2,1,0:T(8,128)(2,1)S(1)} %get-tuple-element.41), channel_id=1, source_target_pairs={{0,1},{1,2},{2,3},{3,4},{4,5},{5,6},{6,7},{7,0},{8,16},{9,17},{10,... | collective-permute-start | bytes 3145736 | tf_op jit(solution)/shard_map/ppermute | solution.py:45
  9.8 6.6 %collective-permute-start = (f32[384,256]{1,0:T(8,128)S(1)}, f32[384,256]{1,0:T(8,128)S(1)}, u32[]{:S(2)}, u32[]{:S(2)}) collective-permute-start(f32[384,256]{1,0:T(8,128)S(1)} %get-tuple-element.27.own), channel_id=1, source_target_pairs={{0,8},{1,9},{2,10},{3,11},{4,12},{5,13},{6,14},{7,15},{8,0},{9,1},... | collective-permute-start | bytes 1179656 | tf_op jit(solution)/shard_map/ppermute | solution.py:45
  10.1 13.1 %collective-permute-start.3 = (bf16[256,512]{1,0:T(8,128)(2,1)S(1)}, bf16[256,512]{1,0:T(8,128)(2,1)S(1)}, u32[]{:S(2)}, u32[]{:S(2)}) collective-permute-start(bf16[256,512]{1,0:T(8,128)(2,1)S(1)} %get-tuple-element.29.x0), channel_id=1, source_target_pairs={{0,7},{1,0},{2,1},{3,2},{4,3},{5,4},{6,5},{7,6},{8,15},{9,8},{10,9... | collective-permute-start | bytes 786440 | tf_op jit(solution)/shard_map/ppermute | solution.py:45
  17.5 5.9 %collective-permute-start.2 = (f32[192,256]{1,0:T(8,128)S(1)}, f32[192,256]{1,0:T(8,128)S(1)}, u32[]{:S(2)}, u32[]{:S(2)}) collective-permute-start(f32[192,256]{1,0:T(8,128)S(1)} %shard_map.97), channel_id=1, source_target_pairs={{0,1},{1,0},{2,3},{3,2},{4,5},{5,4},{6,7},{7,6},{8,9},{9,8},{10,11... | collective-permute-start | bytes 589832 | tf_op jit(solution)/shard_map/ppermute | solution.py:45
  23.5 10.0 %collective-permute-start.5 = (f32[192,256]{1,0:T(8,128)S(1)}, f32[192,256]{1,0:T(8,128)S(1)}, u32[]{:S(2)}, u32[]{:S(2)}) collective-permute-start(f32[192,256]{1,0:T(8,128)S(1)} %add.3.own), channel_id=1, source_target_pairs={{0,16},{1,17},{2,18},{3,19},{4,20},{5,21},{6,22},{7,23},{8,24},{9,... | collective-permute-start | bytes 589832 | tf_op jit(solution)/shard_map/ppermute | solution.py:45
  24.8 11.3 %collective-permute-start.6 = (bf16[256,512]{1,0:T(8,128)(2,1)S(1)}, bf16[256,512]{1,0:T(8,128)(2,1)S(1)}, u32[]{:S(2)}, u32[]{:S(2)}) collective-permute-start(bf16[256,512]{1,0:T(8,128)(2,1)S(1)} %collective-permute-done.3.n), channel_id=1, source_target_pairs={{0,8},{1,9},{2,10},{3,11},{4,12},{5,13},{6,14},{7,15},{8,0},{9,1},... | collective-permute-start | bytes 786440 | tf_op jit(solution)/shard_map/ppermute | solution.py:45
  26.8 9.3 %collective-permute-start.7 = (bf16[256,512]{1,0:T(8,128)(2,1)S(1)}, bf16[256,512]{1,0:T(8,128)(2,1)S(1)}, u32[]{:S(2)}, u32[]{:S(2)}) collective-permute-start(bf16[256,512]{1,0:T(8,128)(2,1)S(1)} %collective-permute-done.3.n), channel_id=1, source_target_pairs={{0,1},{1,2},{2,3},{3,4},{4,5},{5,6},{6,7},{7,0},{8,16},{9,17},{10,... | collective-permute-start | bytes 786440 | tf_op jit(solution)/shard_map/ppermute | solution.py:45
  33.6 12.1 %collective-permute-start.8 = (bf16[256,512]{1,0:T(8,128)(2,1)S(1)}, bf16[256,512]{1,0:T(8,128)(2,1)S(1)}, u32[]{:S(2)}, u32[]{:S(2)}) collective-permute-start(bf16[256,512]{1,0:T(8,128)(2,1)S(1)} %shard_map.100), channel_id=1, source_target_pairs={{0,1},{1,2},{2,3},{3,4},{4,5},{5,6},{6,7},{7,0},{8,9},{9,10},{10,1... | collective-permute-start | bytes 786440 | tf_op jit(solution)/shard_map/ppermute | solution.py:45

commit v4 on v3

--- a/solution.py
+++ b/solution.py
@@ -12,7 +12,7 @@
 SMEM = pl.BlockSpec(memory_space=pltpu.SMEM)
 PANEL = 32
 PIECE = 16
-FIRST_ROWS = 160
+FIRST_ROWS = 192
 
 
 def dot(a, b, dims, precision=lax.Precision.HIGHEST):
@@ -163,17 +163,23 @@
     u[:, 0:FIRST_ROWS, :] = u_first[...]
     w[:, 0:FIRST_ROWS, :] = w_first[...]
     reads = [lambda r, c, m=m: gram[m, r, c] for m in range(2)]
+
+    def orthogonal(first, last):
+        for leaf in range(2):
+            rest = w[leaf, first:last, 0:last]
+            total = None
+            for _ in range(3):
+                part = rest.astype(BF16)
+                rest = rest - part.astype(F32)
+                term = bf_nt(basis[0, leaf, :, 0:last], part)
+                total = term if total is None else total + term
+            q[0, leaf, :, first:last] = total.astype(BF16)
+
     for k in range(FIRST_ROWS, n, PANEL):
         factor_rows(k, reads, [u.at[m] for m in range(2)], [w.at[m] for m in range(2)], n)
-    for leaf in range(2):
-        rest = w[leaf]
-        total = None
-        for _ in range(3):
-            part = rest.astype(BF16)
-            rest = rest - part.astype(F32)
-            term = bf_nt(basis[0, leaf], part)
-            total = term if total is None else total + term
-        q[0, leaf] = total.astype(BF16)
+        if k == FIRST_ROWS:
+            orthogonal(0, n // 2)
+    orthogonal(n // 2, n)
 
 
 def slot_of(slots, leaf, direction):

time: 46.8 us -> 46.8 us (level)
  starting transfers between devices: 16.1 us -> 15.2 us
  waiting for transfers between devices: 1.06 us -> 1.81 us
    pallas_call x1, Pallas kernels: 5.33 us -> 6.54 us  [shards(): u, w = call(leaf_kernel, (firsts, firsts), [VMEM], (VMEM, VMEM))(gram)]
    pallas_call x1, Pallas kernels: 5.1 us -> 4.04 us  [shards(): call(orthogonal_kernel, shape(*basis.shape), [VMEM] * 4, VMEM, [square, s...]
    ppermute x9, starting transfers between devices: 16.1 us -> 15.2 us  [send(): return lax.ppermute(block, axes, route)]
    ppermute x9, waiting for transfers between devices: 1.06 us -> 1.81 us  [send(): return lax.ppermute(block, axes, route)]
  transfers between devices with their start and end apart: 9 -> 9, of which waited for: 2 -> 1; matrix products, arithmetic and copies ran while one was open for 0% -> 0% of each run, Pallas kernels for 47% -> 47%
where the time goes in v4:
time: 46.8 us; the launch traced here: 46.7 us
  Pallas kernels  28.8 us (62%)
  starting transfers between devices  15.2 us (32%)
  waiting for transfers between devices  1.81 us (4%)
  between operations  0.94 us (2%)
    ppermute x9, starting transfers between devices, send(): return lax.ppermute(block, axes, route)  15.2 us
    pallas_call x1, Pallas kernels, shards(): call(near_top_kernel, (shape(*points_x.shape), wide, shape(1, 1, rank, ra...  8.83 us
    pallas_call x1, Pallas kernels, shards(): u, w = call(leaf_kernel, (firsts, firsts), [VMEM], (VMEM, VMEM))(gram)  6.54 us
    pallas_call x1, Pallas kernels, shards(): call(first_kernel, (shape(2, rank, rank, dtype=F32), shape(rank + half, r...  5.8 us
    pallas_call x1, Pallas kernels, shards(): call(orthogonal_kernel, shape(*basis.shape), [VMEM] * 4, VMEM, [square, s...  4.04 us
    ppermute x9, waiting for transfers between devices, send(): return lax.ppermute(block, axes, route)  1.81 us
    pallas_call x1, Pallas kernels, shards(): call(own_kernel, (wide, wide, wide), [SMEM, *[VMEM] * 4], (VMEM, VMEM, VM...  1.43 us
    pallas_call x1, Pallas kernels, shards(): call(node_kernel, packed, [VMEM] * 2, VMEM, [pltpu.VMEM((rank, rank), F32)])  1.14 us
  transfers between devices with their start and end apart: 9, of which 1 were waited for; matrix products, arithmetic and copies ran while one was open for 0% of the time, Pallas kernels for 47%

profile of v4, /device:TPU:1, one launch (start us, length us, event | category | flops | bytes accessed | tf_op | source)
XLA Modules:
  0.0 46.7 jit_solution(11825386164234945462)
XLA Ops:
  0.6 0.0 copy-start.2
  0.6 0.0 copy-start.3
  0.7 0.0 copy-start
  0.7 5.8 %shard_map.94 = (f32[2,256,256]{2,1,0:T(8,128)S(1)}, f32[384,256]{1,0:T(8,128)S(1)}, bf16[256,512]{1,0:T(8,128)(2,1)S(1)}, bf16[4,256,512]{2,1,0:T(8,128)(2,1)S(1)}, bf16[4,256,512]{2,1,0:T(8,128)(2,1)S(1)}) custom-call(bf16[1,2,512,256]{3,2,1,0:T(8,128)(2,1)} %basis.1, f32[1,2,256,256]{3,2,1,0:T(8,128)} %transfer_h.1, f32[1,1,128,256]{3,2,1,0:T(8,128)} %node_h.1, ...), custom_call_target="tpu_custom_call" | custom-call | flops 1000000 | bytes 1024 | tf_op jit(solution)/shard_map/pallas_call | solution.py:384
  6.5 0.0 copy-start.1
  6.5 3.3 %collective-permute-start.1 = (bf16[4,256,512]{2,1,0:T(8,128)(2,1)S(1)}, bf16[4,256,512]{2,1,0:T(8,128)(2,1)S(1)}, u32[]{:S(2)}, u32[]{:S(2)}) collective-permute-start(bf16[4,256,512]{2,1,0:T(8,128)(2,1)S(1)} %get-tuple-element.28.gx_a), channel_id=1, source_target_pairs={{0,8},{1,9},{2,10},{3,11},{4,12},{5,13},{6,14},{7,15},{8,0},{9,1},... | collective-permute-start | bytes 3145736 | tf_op jit(solution)/shard_map/ppermute | solution.py:45
  9.8 0.0 collective-permute-start.4
  9.8 0.3 collective-permute-start
  10.1 4.8 %collective-permute-start.3 = (bf16[256,512]{1,0:T(8,128)(2,1)S(1)}, bf16[256,512]{1,0:T(8,128)(2,1)S(1)}, u32[]{:S(2)}, u32[]{:S(2)}) collective-permute-start(bf16[256,512]{1,0:T(8,128)(2,1)S(1)} %get-tuple-element.29.x0), channel_id=1, source_target_pairs={{0,7},{1,0},{2,1},{3,2},{4,3},{5,4},{6,5},{7,6},{8,15},{9,8},{10,9... | collective-permute-start | bytes 786440 | tf_op jit(solution)/shard_map/ppermute | solution.py:45
  14.9 0.0 copy-done.2
  14.9 0.0 copy-done.3
  14.9 0.0 copy-done
  14.9 1.4 %shard_map.95 = (f32[256,512]{1,0:T(8,128)S(1)}, f32[256,512]{1,0:T(8,128)S(1)}, f32[256,512]{1,0:T(8,128)S(1)}) custom-call(s32[1,2,5]{2,1,0:T(2,128)S(1)} %copy-done.3, f32[1,5,2,512]{3,2,1,0:T(2,128)S(1)} %bitcast.2, bf16[1,2,5,512,512]{4,3,2,1,0:T(8,128)(2,1)S(1)} %copy-done, bf16[256,512]{1,0:T(8,128)(2,1)S(1)} %get-tuple-element.29.x0, ...), custom_call_target="tpu_custom_call" | custom-call | flops 2000000000 | bytes 1024 | tf_op jit(solution)/shard_map/pallas_call | solution.py:412
  16.4 0.0 collective-permute-done.other
  16.4 0.0 collective-permute-done.1.gx_a.a
  16.4 1.1 %shard_map.97 = f32[192,256]{1,0:T(8,128)S(1)} custom-call(f32[384,256]{1,0:T(8,128)S(1)} %get-tuple-element.27.own, f32[384,256]{1,0:T(8,128)S(1)} %collective-permute-done.other), custom_call_target="tpu_custom_call" | custom-call | flops 1000000 | bytes 1024 | tf_op jit(solution)/shard_map/pallas_call | solution.py:416
  17.5 0.3 collective-permute-start.2
  17.8 6.5 %shard_map.96 = (f32[2,192,256]{2,1,0:T(8,128)S(1)}, f32[2,192,256]{2,1,0:T(8,128)S(1)}) custom-call(f32[2,256,256]{2,1,0:T(8,128)S(1)} %get-tuple-element.34.gram), custom_call_target="tpu_custom_call" | custom-call | flops 1000000 | bytes 1024 | tf_op jit(solution)/shard_map/pallas_call | solution.py:426
  24.4 0.0 collective-permute-done.3.n
  24.4 0.0 collective-permute-done.2
  24.4 1.4 %collective-permute-start.5 = (f32[192,256]{1,0:T(8,128)S(1)}, f32[192,256]{1,0:T(8,128)S(1)}, u32[]{:S(2)}, u32[]{:S(2)}) collective-permute-start(f32[192,256]{1,0:T(8,128)S(1)} %add.3.own), channel_id=1, source_target_pairs={{0,16},{1,17},{2,18},{3,19},{4,20},{5,21},{6,22},{7,23},{8,24},{9,... | collective-permute-start | bytes 589832 | tf_op jit(solution)/shard_map/ppermute | solution.py:45
  25.8 1.1 %collective-permute-start.6 = (bf16[256,512]{1,0:T(8,128)(2,1)S(1)}, bf16[256,512]{1,0:T(8,128)(2,1)S(1)}, u32[]{:S(2)}, u32[]{:S(2)}) collective-permute-start(bf16[256,512]{1,0:T(8,128)(2,1)S(1)} %collective-permute-done.3.n), channel_id=1, source_target_pairs={{0,8},{1,9},{2,10},{3,11},{4,12},{5,13},{6,14},{7,15},{8,0},{9,1},... | collective-permute-start | bytes 786440 | tf_op jit(solution)/shard_map/ppermute | solution.py:45
  26.9 1.5 %collective-permute-start.7 = (bf16[256,512]{1,0:T(8,128)(2,1)S(1)}, bf16[256,512]{1,0:T(8,128)(2,1)S(1)}, u32[]{:S(2)}, u32[]{:S(2)}) collective-permute-start(bf16[256,512]{1,0:T(8,128)(2,1)S(1)} %collective-permute-done.3.n), channel_id=1, source_target_pairs={{0,1},{1,2},{2,3},{3,4},{4,5},{5,6},{6,7},{7,0},{8,16},{9,17},{10,... | collective-permute-start | bytes 786440 | tf_op jit(solution)/shard_map/ppermute | solution.py:45
  28.4 0.0 copy-done.1
  28.4 4.0 %shard_map.98 = bf16[1,2,512,256]{3,2,1,0:T(8,128)(2,1)} custom-call(f32[2,256,256]{2,1,0:T(8,128)S(1)} %get-tuple-element.34.gram, bf16[1,2,512,256]{3,2,1,0:T(8,128)(2,1)S(1)} %copy-done.1, f32[2,192,256]{2,1,0:T(8,128)S(1)} %get-tuple-element.39.u_first, f32[2,192,256]{2,1,0:T(8,128)S(1)} %get-tuple-element.40.w_first), custom_call_target="tpu_custom_call" | custom-call | flops 1000000 | bytes 1024 | tf_op jit(solution)/shard_map/pallas_call | solution.py:435
  32.4 0.0 collective-permute-done.4.gx_b.b
  32.4 0.0 collective-permute-done.5.other
  32.4 0.1 shard_map.100
  32.5 2.5 %collective-permute-start.8 = (bf16[256,512]{1,0:T(8,128)(2,1)S(1)}, bf16[256,512]{1,0:T(8,128)(2,1)S(1)}, u32[]{:S(2)}, u32[]{:S(2)}) collective-permute-start(bf16[256,512]{1,0:T(8,128)(2,1)S(1)} %shard_map.100), channel_id=1, source_target_pairs={{0,1},{1,2},{2,3},{3,4},{4,5},{5,6},{6,7},{7,0},{8,9},{9,10},{10,1... | collective-permute-start | bytes 786440 | tf_op jit(solution)/shard_map/ppermute | solution.py:45
  35.0 0.0 collective-permute-done.6.n_a
  35.0 0.0 collective-permute-done.7.n_b
  35.1 8.8 %shard_map.99 = (bf16[1,2,512,256]{3,2,1,0:T(8,128)(2,1)}, f32[256,512]{1,0:T(8,128)S(1)}, f32[1,1,256,256]{3,2,1,0:T(8,128)}) custom-call(s32[1,2,5]{2,1,0:T(2,128)S(1)} %copy-done.3, f32[1,5,2,512]{3,2,1,0:T(2,128)S(1)} %bitcast.3, bf16[1,2,5,512,512]{4,3,2,1,0:T(8,128)(2,1)S(1)} %copy-done, f32[256,512]{1,0:T(8,128)S(1)} %get-tuple-element.31.low_in, ...), custom_call_target="tpu_custom_call" | custom-call | flops 1000000 | bytes 1024 | tf_op jit(solution)/shard_map/pallas_call | solution.py:441
  43.9 1.8 %collective-permute-done.8.south = bf16[256,512]{1,0:T(8,128)(2,1)S(1)} collective-permute-done((bf16[256,512]{1,0:T(8,128)(2,1)S(1)}, bf16[256,512]{1,0:T(8,128)(2,1)S(1)}, u32[]{:S(2)}, u32[]{:S(2)}) %collective-permute-start.8) | collective-permute-done | bytes 262176 | tf_op jit(solution)/shard_map/ppermute | solution.py:45
  45.7 0.9 %shard_map.101 = bf16[1,2,512,256]{3,2,1,0:T(8,128)(2,1)} custom-call(bf16[1,2,512,256]{3,2,1,0:T(8,128)(2,1)} %get-tuple-element.46.near, f32[256,512]{1,0:T(8,128)S(1)} %get-tuple-element.47.low, bf16[256,512]{1,0:T(8,128)(2,1)S(1)} %collective-permute-done.8.south), custom_call_target="tpu_custom_call", output_to_operand_aliasing={{}: (0, {})} | custom-call | flops 1000000 | bytes 1024 | tf_op jit(solution)/shard_map/pallas_call | solution.py:448
  (1 shorter events, 0.0 us)
Async XLA Ops:
  0.6 14.3 %copy-start.2 = (f32[1,2,5,512]{3,1,2,0:T(2,128)S(1)}, f32[1,2,5,512]{3,1,2,0:T(2,128)}, u32[]{:S(2)}) copy-start(f32[1,2,5,512]{3,1,2,0:T(2,128)} %param.9) | copy-start | bytes 61444
  0.6 14.3 %copy-start.3 = (s32[1,2,5]{2,1,0:T(2,128)S(1)}, s32[1,2,5]{2,1,0:T(2,128)}, u32[]{:S(2)}) copy-start(s32[1,2,5]{2,1,0:T(2,128)} %slots.3) | copy-start | bytes 124
  0.7 14.3 %copy-start = (bf16[1,2,5,512,512]{4,3,2,1,0:T(8,128)(2,1)S(1)}, bf16[1,2,5,512,512]{4,3,2,1,0:T(8,128)(2,1)}, u32[]{:S(2)}) copy-start(bf16[1,2,5,512,512]{4,3,2,1,0:T(8,128)(2,1)} %tiles.3) | copy-start | bytes 15728644
  6.5 21.9 %copy-start.1 = (bf16[1,2,512,256]{3,2,1,0:T(8,128)(2,1)S(1)}, bf16[1,2,512,256]{3,2,1,0:T(8,128)(2,1)}, u32[]{:S(2)}) copy-start(bf16[1,2,512,256]{3,2,1,0:T(8,128)(2,1)} %basis.1) | copy-start | bytes 1572868
  6.5 9.9 %collective-permute-start.1 = (bf16[4,256,512]{2,1,0:T(8,128)(2,1)S(1)}, bf16[4,256,512]{2,1,0:T(8,128)(2,1)S(1)}, u32[]{:S(2)}, u32[]{:S(2)}) collective-permute-start(bf16[4,256,512]{2,1,0:T(8,128)(2,1)S(1)} %get-tuple-element.28.gx_a), channel_id=1, source_target_pairs={{0,8},{1,9},{2,10},{3,11},{4,12},{5,13},{6,14},{7,15},{8,0},{9,1},... | collective-permute-start | bytes 3145736 | tf_op jit(solution)/shard_map/ppermute | solution.py:45
  9.8 22.6 %collective-permute-start.4 = (bf16[4,256,512]{2,1,0:T(8,128)(2,1)S(1)}, bf16[4,256,512]{2,1,0:T(8,128)(2,1)S(1)}, u32[]{:S(2)}, u32[]{:S(2)}) collective-permute-start(bf16[4,256,512]{2,1,0:T(8,128)(2,1)S(1)} %get-tuple-element.41), channel_id=1, source_target_pairs={{0,1},{1,2},{2,3},{3,4},{4,5},{5,6},{6,7},{7,0},{8,16},{9,17},{10,... | collective-permute-start | bytes 3145736 | tf_op jit(solution)/shard_map/ppermute | solution.py:45
  9.8 6.6 %collective-permute-start = (f32[384,256]{1,0:T(8,128)S(1)}, f32[384,256]{1,0:T(8,128)S(1)}, u32[]{:S(2)}, u32[]{:S(2)}) collective-permute-start(f32[384,256]{1,0:T(8,128)S(1)} %get-tuple-element.27.own), channel_id=1, source_target_pairs={{0,8},{1,9},{2,10},{3,11},{4,12},{5,13},{6,14},{7,15},{8,0},{9,1},... | collective-permute-start | bytes 1179656 | tf_op jit(solution)/shard_map/ppermute | solution.py:45
  10.1 14.3 %collective-permute-start.3 = (bf16[256,512]{1,0:T(8,128)(2,1)S(1)}, bf16[256,512]{1,0:T(8,128)(2,1)S(1)}, u32[]{:S(2)}, u32[]{:S(2)}) collective-permute-start(bf16[256,512]{1,0:T(8,128)(2,1)S(1)} %get-tuple-element.29.x0), channel_id=1, source_target_pairs={{0,7},{1,0},{2,1},{3,2},{4,3},{5,4},{6,5},{7,6},{8,15},{9,8},{10,9... | collective-permute-start | bytes 786440 | tf_op jit(solution)/shard_map/ppermute | solution.py:45
  17.5 6.8 %collective-permute-start.2 = (f32[192,256]{1,0:T(8,128)S(1)}, f32[192,256]{1,0:T(8,128)S(1)}, u32[]{:S(2)}, u32[]{:S(2)}) collective-permute-start(f32[192,256]{1,0:T(8,128)S(1)} %shard_map.97), channel_id=1, source_target_pairs={{0,1},{1,0},{2,3},{3,2},{4,5},{5,4},{6,7},{7,6},{8,9},{9,8},{10,11... | collective-permute-start | bytes 589832 | tf_op jit(solution)/shard_map/ppermute | solution.py:45
  24.4 8.0 %collective-permute-start.5 = (f32[192,256]{1,0:T(8,128)S(1)}, f32[192,256]{1,0:T(8,128)S(1)}, u32[]{:S(2)}, u32[]{:S(2)}) collective-permute-start(f32[192,256]{1,0:T(8,128)S(1)} %add.3.own), channel_id=1, source_target_pairs={{0,16},{1,17},{2,18},{3,19},{4,20},{5,21},{6,22},{7,23},{8,24},{9,... | collective-permute-start | bytes 589832 | tf_op jit(solution)/shard_map/ppermute | solution.py:45
  25.8 9.3 %collective-permute-start.6 = (bf16[256,512]{1,0:T(8,128)(2,1)S(1)}, bf16[256,512]{1,0:T(8,128)(2,1)S(1)}, u32[]{:S(2)}, u32[]{:S(2)}) collective-permute-start(bf16[256,512]{1,0:T(8,128)(2,1)S(1)} %collective-permute-done.3.n), channel_id=1, source_target_pairs={{0,8},{1,9},{2,10},{3,11},{4,12},{5,13},{6,14},{7,15},{8,0},{9,1},... | collective-permute-start | bytes 786440 | tf_op jit(solution)/shard_map/ppermute | solution.py:45
  26.9 8.2 %collective-permute-start.7 = (bf16[256,512]{1,0:T(8,128)(2,1)S(1)}, bf16[256,512]{1,0:T(8,128)(2,1)S(1)}, u32[]{:S(2)}, u32[]{:S(2)}) collective-permute-start(bf16[256,512]{1,0:T(8,128)(2,1)S(1)} %collective-permute-done.3.n), channel_id=1, source_target_pairs={{0,1},{1,2},{2,3},{3,4},{4,5},{5,6},{6,7},{7,0},{8,16},{9,17},{10,... | collective-permute-start | bytes 786440 | tf_op jit(solution)/shard_map/ppermute | solution.py:45
  32.5 13.1 %collective-permute-start.8 = (bf16[256,512]{1,0:T(8,128)(2,1)S(1)}, bf16[256,512]{1,0:T(8,128)(2,1)S(1)}, u32[]{:S(2)}, u32[]{:S(2)}) collective-permute-start(bf16[256,512]{1,0:T(8,128)(2,1)S(1)} %shard_map.100), channel_id=1, source_target_pairs={{0,1},{1,2},{2,3},{3,4},{4,5},{5,6},{6,7},{7,0},{8,9},{9,10},{10,1... | collective-permute-start | bytes 786440 | tf_op jit(solution)/shard_map/ppermute | solution.py:45
